TPU v7x, 256 devices: a whole 4x4x8 slice. The times are simulated.
256 devices in a mesh: dp: 8 (over z), shard: 32 (over y, x, core).
Axes of the slice: x: 4, y: 4, z: 8, core: 2. Of those that a mesh axis runs over, the one named last changes fastest.
Arguments:
- grads: bfloat16 [8, 64, 1024, 1024], P('dp', None, 'shard')
- left_factor: bfloat16 [256, 1024, 1024], P(('dp', 'shard'))
- right_factor: bfloat16 [256, 1024, 1024], P(('dp', 'shard'))
- momentum: bfloat16 [256, 1024, 1024], P(('dp', 'shard')), may hold values from -3 to 3
- block_order: int32 [64], replicated, may hold values from 0 to 63, each once
- owner_counts: int32 [32], replicated, may hold values from 1 to 8, 64 in all
Outputs:
- update: bfloat16 [64, 1024, 1024], P(None, 'shard', 'dp')
- new_momentum: bfloat16 [256, 1024, 1024], P(('dp', 'shard'))
Inputs may be any that keep to these rules, and one draw needn't show every extreme that they name: Owner group o takes the owner_counts[o] entries of block_order after those of groups 0 to o - 1; its j-th block lives in slot j * 32 + o. `owner_counts`: the counts sum to 64; some group takes 8 blocks.
All inputs are finite; a program needn't handle non-finite values.
Results may differ from a plain program's by a relative error of at most 0.02.
Values may be sent and summed in bfloat16 or wider, within the bound.
A program may use at most 128 MiB of HBM per device.

v0:
```python
import jax
import jax.numpy as jnp
from jax import lax
from jax.sharding import PartitionSpec as P

decay_rate = 0.9
learn_rate = 0.8


def slot_table(owner_counts, block_order, dp_count):
    finish = jnp.cumsum(owner_counts)
    starts = finish - owner_counts
    within = jnp.arange(dp_count, dtype=jnp.int32)
    position = starts[:, None] + within[None, :]
    filled = within[None, :] < owner_counts[:, None]
    placed = jnp.where(filled, position, -1)
    listing = jnp.arange(block_order.shape[0], dtype=jnp.int32)
    matches = placed[:, :, None] == listing[None, None, :]
    block_ids = jnp.sum(jnp.where(matches, block_order[None, None, :], 0), axis=2)
    return (block_ids, filled)


def per_device(grads, left_factor, right_factor, momentum, block_order, owner_counts):
    summed = lax.psum_scatter(grads, "dp", scatter_dimension=3, tiled=True).astype(jnp.float32)
    pieces = summed[0].astype(jnp.bfloat16)
    total_blocks = pieces.shape[0]
    groups = lax.axis_size("shard")
    dp_count = lax.axis_size("dp")
    block_ids, filled = slot_table(owner_counts, block_order, dp_count)
    flat_ids = block_ids.reshape(-1)
    flat_filled = filled.reshape(-1)
    outgoing = jnp.take(pieces, flat_ids, axis=0)
    outgoing = jnp.where(flat_filled[:, None, None], outgoing, jnp.zeros_like(outgoing))
    outgoing = outgoing.reshape(groups, dp_count, pieces.shape[1], pieces.shape[2])
    widened = pieces.astype(jnp.float32)
    grand_total = lax.psum(jnp.sum(widened * widened), ("dp", "shard"))
    arrived = lax.all_to_all(
        lax.all_to_all(outgoing, "dp", split_axis=1, concat_axis=3, tiled=True),
        "shard",
        split_axis=0,
        concat_axis=2,
        tiled=True,
    )
    grad_block = arrived[0, 0]
    inner_prod = jnp.dot(left_factor[0], grad_block, preferred_element_type=jnp.float32).astype(
        jnp.bfloat16
    )
    outer_prod = jnp.dot(inner_prod, right_factor[0], preferred_element_type=jnp.float32)
    grad_wide = grad_block.astype(jnp.float32)
    own_square = jnp.sum(grad_wide * grad_wide)
    cell_count = grad_block.shape[0] * grad_block.shape[1]
    graft_scale = jnp.sqrt(own_square / cell_count) * lax.rsqrt(
        jnp.mean(outer_prod * outer_prod) + 1e-06
    )
    clip_scale = jnp.minimum(
        1.0, 0.5 * lax.rsqrt(grand_total / (total_blocks * cell_count) + 1e-06)
    )
    direction = clip_scale * (graft_scale * outer_prod)
    momentum_next = decay_rate * momentum[0].astype(jnp.float32) + direction
    new_momentum = momentum_next.astype(jnp.bfloat16)[None]
    update_block = (-learn_rate * (decay_rate * momentum_next + direction)).astype(jnp.bfloat16)
    sending = update_block[None, None]
    returned = lax.all_to_all(
        lax.all_to_all(sending, "dp", split_axis=3, concat_axis=1, tiled=True),
        "shard",
        split_axis=2,
        concat_axis=0,
        tiled=True,
    )
    flat_back = returned.reshape(groups * dp_count, returned.shape[2], returned.shape[3])
    listing = jnp.arange(total_blocks, dtype=jnp.int32)
    slot_range = jnp.arange(groups * dp_count, dtype=jnp.int32)
    matches = (flat_ids[None, :] == listing[:, None]) & flat_filled[None, :]
    slot_index = jnp.sum(jnp.where(matches, slot_range[None, :], 0), axis=1)
    update = jnp.take(flat_back, slot_index, axis=0)
    return (update, new_momentum)


def solution(mesh):
    placed = (
        P("dp", None, "shard", None),
        P(("dp", "shard"), None, None),
        P(("dp", "shard"), None, None),
        P(("dp", "shard"), None, None),
        P(),
        P(),
    )
    return jax.shard_map(
        per_device,
        mesh=mesh,
        in_specs=placed,
        out_specs=(P(None, "shard", "dp"), P(("dp", "shard"), None, None)),
        check_vma=False,
    )
```

profile of v0, /device:TPU:1, one launch (start us, length us, event | category | flops | bytes accessed | tf_op | source)
XLA Modules:
  0.0 436.4 jit_solution(13786708729809633621)
XLA Ops:
  7.2 0.0 copy-start
  7.2 0.0 reduce-scatter.4.cloned.1.call-start
  7.2 23.2 %copy.45 = bf16[1,64,32,1024]{2,1,0,3:T(8,128)(2,1)} copy(bf16[1,64,32,1024]{3,2,1,0:T(8,128)(2,1)} %param.6) | data formatting | bytes 8388608
  30.4 22.6 %reshape.192 = bf16[1024,2048]{1,0:T(8,128)(2,1)} reshape(bf16[1024,1,64,32]{3,2,1,0:T(8,128)(2,1)} %bitcast.64) | data formatting | bytes 8388608
  53.0 0.0 reduce-scatter.4.cloned.1.call-update
  53.0 0.6 copy-done.2
  53.7 0.1 copy.35
  53.7 0.1 reduce-window.9
  53.8 0.1 reduce.1
  53.9 0.1 add_select_fusion
  54.0 0.0 copy-done.3
  54.0 0.7 select_reduce_fusion
  54.7 0.1 reshape.174
  54.8 0.1 copy.37
  54.9 0.1 iota_compare_fusion.2
  55.0 0.1 copy.36
  55.1 57.3 %reduce-scatter.4.cloned.1.call-done = bf16[128,2048]{1,0:T(8,128)(2,1)} async-done(((bf16[1024,2048]{1,0:T(8,128)(2,1)}), bf16[128,2048]{1,0:T(8,128)(2,1)}) %reduce-scatter.4.cloned.1.call-update) | async-done | bytes 524304
  112.3 3.5 reshape.193
  115.9 3.2 copy.46
  119.1 2.2 gather_fusion
  121.3 2.8 fusion.7
  124.0 53.7 %all_to_all.60 = bf16[32,8,32,128]{3,2,0,1:T(8,128)(2,1)S(1)} all-to-all(bf16[32,8,32,128]{3,2,0,1:T(8,128)(2,1)S(1)} %fusion.7), channel_id=1, replica_groups=mesh['dp'=8,'shard'=32] {'dp'}, dimensions={1} | all-to-all | bytes 4194304 | tf_op jit(solution)/shard_map/all_to_all | solution.py:38
  177.7 1.7 bitcast_bitcast_fusion
  179.4 9.3 %all-to-all-start.1 = ((bf16[32,1,32,1024]{3,2,1,0:T(8,128)(2,1)}), bf16[32,1,32,1024]{3,2,1,0:T(8,128)(2,1)}, u32[]{:S(2)}, u32[]{:S(2)}) async-start(bf16[32,1,32,1024]{3,2,1,0:T(8,128)(2,1)} %bitcast_bitcast_fusion), calls=%async_computation.1 | async-start | bytes 4194304 | tf_op jit(solution)/shard_map/all_to_all | solution.py:37
  188.7 0.9 multiply_reduce_fusion.2
  189.5 92.1 %psum.7 = f32[]{:T(128)} all-reduce(f32[]{:T(128)} %multiply_reduce_fusion.2), channel_id=1, replica_groups=mesh['dp'=8,'shard'=32] {'dp','shard'}, use_global_device_ids=true, to_apply=%region_5.6 | all-reduce | flops 1 | bytes 8 | tf_op jit(solution)/shard_map/psum | solution.py:36
  282.3 0.0 all-to-all-done.1
  282.3 3.3 multiply_reduce_fusion.1
  286.3 9.4 %multiply_reduce_fusion = (f32[]{:T(128)}, f32[1024,1024]{1,0:T(8,128)}) fusion(bf16[1,1024,1024]{2,1,0:T(8,128)(2,1)S(1)} %copy-done, bf16[1024,1024]{1,0:T(8,128)(2,1)} %bitcast.8, bf16[1,1024,1024]{2,1,0:T(8,128)(2,1)} %param.7), kind=kOutput, calls=%fused_computation.5 | convolution fusion | flops 4298113024 | bytes 10485764 | tf_op jit(solution)/shard_map/dot_general | solution.py:48
  296.4 5.5 %fusion.1 = (bf16[1,1024,1024]{2,1,0:T(8,128)(2,1)}, bf16[1,1,1024,1024]{3,2,1,0:T(8,128)(2,1)S(1)}) fusion(f32[1024,1024]{1,0:T(8,128)} %get-tuple-element.5, bf16[1,1024,1024]{2,1,0:T(8,128)(2,1)} %param.9, f32[]{:T(128)S(6)} %mul.46, f32[]{:T(128)S(6)} %min_shard_map.3), kind=kLoop, calls=%fused_computation.8 | loop fusion | flops 10485760 | bytes 10485768 | tf_op jit(solution)/shard_map/broadcast_in_dim | solution.py:60
  301.9 7.7 %copy.41 = bf16[1,1,1024,1024]{2,1,0,3:T(2,128)(2,1)} copy(bf16[1,1,1024,1024]{3,2,1,0:T(8,128)(2,1)S(1)} %get-tuple-element.3) | data formatting | bytes 4194304 | tf_op jit(solution)/shard_map/broadcast_in_dim | solution.py:62
  309.6 0.5 broadcast.118
  310.1 12.8 %reduce.2 = bf16[1024,1024]{1,0:T(8,128)(2,1)S(1)} reduce(bf16[1024,1,1,1024]{3,2,1,0:T(2,128)(2,1)} %bitcast.66, bf16[]{:T(256)} %broadcast.118), dimensions={1,2}, to_apply=%bitcast.55.reduce_sub_computation | reduce | bytes 4194306
  322.9 3.8 reshape.195
  326.7 53.5 %all_to_all.61 = bf16[8,2,65536]{2,1,0:T(2,128)(2,1)S(1)} all-to-all(bf16[8,2,65536]{2,1,0:T(2,128)(2,1)} %reshape.195), channel_id=1, replica_groups=mesh['dp'=8,'shard'=32] {'dp'}, dimensions={0} | all-to-all | bytes 4194304 | tf_op jit(solution)/shard_map/all_to_all | solution.py:64
  380.2 4.4 %reshape.196 = bf16[1024,1,1,1024]{3,2,1,0:T(2,128)(2,1)} reshape(bf16[8,2,65536]{2,1,0:T(2,128)(2,1)S(1)} %all_to_all.61) | data formatting | bytes 4194304
  384.6 3.0 copy.47
  387.6 2.9 copy.42
  390.6 5.6 %all-to-all-start.3 = ((bf16[1,8,1024,128]{3,1,0,2:T(8,128)(2,1)}), bf16[1,8,1024,128]{3,1,0,2:T(8,128)(2,1)S(1)}, u32[]{:S(2)}, u32[]{:S(2)}) async-start(bf16[1,8,1024,128]{3,1,0,2:T(8,128)(2,1)} %copy.42), calls=%async_computation.3 | async-start | bytes 4194304 | tf_op jit(solution)/shard_map/all_to_all | solution.py:63
  396.2 0.1 eq.31
  396.3 0.1 lt.77
  396.4 0.1 select_reduce_fusion.1
  396.5 27.6 %all-to-all-done.3 = bf16[1,8,1024,128]{3,1,0,2:T(8,128)(2,1)S(1)} async-done(((bf16[1,8,1024,128]{3,1,0,2:T(8,128)(2,1)}), bf16[1,8,1024,128]{3,1,0,2:T(8,128)(2,1)S(1)}, u32[]{:S(2)}, u32[]{:S(2)}) %all-to-all-start.3) | async-done | bytes 2097184 | tf_op jit(solution)/shard_map/all_to_all | solution.py:63
  424.1 0.3 copy.43
  424.4 0.0 copy-start.1
  424.4 2.0 copy.44
  426.4 2.2 gather_fusion.1
  428.6 0.9 broadcast_select_fusion
  (11 shorter events, 0.1 us)
Async XLA Ops:
  7.2 279.1 %copy-start = (bf16[1,1024,1024]{2,1,0:T(8,128)(2,1)S(1)}, bf16[1,1024,1024]{2,1,0:T(8,128)(2,1)}, u32[]{:S(2)}) copy-start(bf16[1,1024,1024]{2,1,0:T(8,128)(2,1)} %param.8) | copy-start | bytes 6291460
  7.2 105.1 %reduce-scatter.4.cloned.1.call-start = ((), (), s32[]{:S(2)}) async-start(), calls=%async_computation.5 | async-start | bytes 4718592
  53.0 0.7 copy-start.2
  53.0 1.0 copy-start.3
  179.4 102.9 %all-to-all-start.1 = ((bf16[32,1,32,1024]{3,2,1,0:T(8,128)(2,1)}), bf16[32,1,32,1024]{3,2,1,0:T(8,128)(2,1)}, u32[]{:S(2)}, u32[]{:S(2)}) async-start(bf16[32,1,32,1024]{3,2,1,0:T(8,128)(2,1)} %bitcast_bitcast_fusion), calls=%async_computation.1 | async-start | bytes 4194304 | tf_op jit(solution)/shard_map/all_to_all | solution.py:37
  390.6 33.6 %all-to-all-start.3 = ((bf16[1,8,1024,128]{3,1,0,2:T(8,128)(2,1)}), bf16[1,8,1024,128]{3,1,0,2:T(8,128)(2,1)S(1)}, u32[]{:S(2)}, u32[]{:S(2)}) async-start(bf16[1,8,1024,128]{3,1,0,2:T(8,128)(2,1)} %copy.42), calls=%async_computation.3 | async-start | bytes 4194304 | tf_op jit(solution)/shard_map/all_to_all | solution.py:63
  424.4 5.2 %copy-start.1 = (bf16[1,1024,1024]{2,1,0:T(8,128)(2,1)S(1)}, bf16[1,1024,1024]{2,1,0:T(8,128)(2,1)}, u32[]{:S(2)}) copy-start(bf16[1,1024,1024]{2,1,0:T(8,128)(2,1)} %param.8) | copy-start | bytes 6291460
Sparse Core Ops, SparseCore 0:
  53.2 59.1 reduce-scatter.3
where the time goes:
time: 438 us; the launch traced here: 436 us
  blocking collectives  199 us (45%)
  waiting for transfers between devices  84.9 us (19%)
  local copies, waits for them, and re-layouts  84.4 us (19%)
  other arithmetic  27.3 us (6%)
  between operations  16.3 us (4%)
  starting transfers between devices  14.9 us (3%)
  matrix products  9.43 us (2%)
    psum x1, blocking collectives, per_device(): grand_total = lax.psum(jnp.sum(widened * widened), ('dp', 'shard'))  92.1 us
    unnamed x16, local copies, waits for them, and re-layouts  64.9 us
    unnamed x2, waiting for transfers between devices  57.3 us
    all_to_all x1, blocking collectives, per_device(): lax.all_to_all(outgoing, 'dp', split_axis=1, concat_axis=3, tiled=True)  53.7 us
    all_to_all x1, blocking collectives, per_device(): lax.all_to_all(sending, 'dp', split_axis=3, concat_axis=1, tiled=True)  53.5 us
    all_to_all x1, waiting for transfers between devices, per_device(): lax.all_to_all(lax.all_to_all(sending, 'dp', split_axis=3, concat_axis=1,...  27.6 us
    unnamed x1, other arithmetic  12.8 us
    dot_general x1, matrix products, per_device(): jnp.dot(inner_prod, right_factor[0], preferred_element_type=jnp.float32)  9.43 us
  transfers between devices with their start and end apart: 3, of which 2 were waited for; matrix products, arithmetic and copies ran while one was open for 1% of the time, Pallas kernels for 0%

commit v1 on v0

v1 whole, which is shorter than its diff:
```python
import functools

import jax
import jax.numpy as jnp
from jax import lax
from jax.experimental import pallas as pl
from jax.experimental.pallas import tpu as pltpu
from jax.sharding import PartitionSpec as P

MESH = pl.DeviceIdType.MESH
LAG = 4
SKEW = 3
F32 = jnp.float32
BF16 = jnp.bfloat16


class Plan:
    def __init__(self, planes, groups, blocks, rows, cols):
        self.planes, self.groups, self.blocks = planes, groups, blocks
        self.rows, self.cols = rows, cols
        extras = blocks - groups
        self.most = [groups] + [
            min(groups, (extras - (planes - 1 - j)) // j) for j in range(1, planes)
        ]
        self.base = [sum(self.most[:j]) for j in range(planes)]
        self.slots = sum(self.most)
        self.sends = max(extras - (planes - 2), LAG) + (planes - 2) * LAG
        self.listed = 2 * (self.sends + LAG)
        place = 0
        for name, size in (
            ("up", self.listed),
            ("down", self.listed),
            ("first", groups),
            ("rank", groups),
            ("slot", groups),
            ("where", blocks),
            ("spare", 1),
            ("scalars", 16),
        ):
            setattr(self, name, place)
            place += size
        self.size = place


def table_kernel(plan, order_ref, counts_ref, tab, held):
    n, g = plan.planes, plan.groups
    me, col = lax.axis_index("dp"), lax.axis_index("shard")
    prev, nxt = lax.rem(me + n - 1, n), lax.rem(me + 1, n)

    def clear(i, c):
        tab[i] = 0
        return c

    lax.fori_loop(0, plan.size, clear, 0)
    hist, desc, asc, rank, base, width = 0, 16, 32, 48, 64, 80
    for i in range(16):
        held[hist + i] = 0
        held[rank + i] = 0

    def tally(o, c):
        k = counts_ref[o]
        held[hist + k] = held[hist + k] + 1
        return c

    lax.fori_loop(0, g, tally, 0)
    run = jnp.int32(0)
    down_at = jnp.int32(0)
    widths = [None] * n
    for j in range(n - 1, -1, -1):
        run = run + held[hist + j + 1]
        widths[j] = jnp.int32(LAG) if j == 0 else jnp.maximum(run, LAG)
        held[desc + j] = down_at
        held[width + j] = widths[j]
        held[base + j] = plan.base[j]
        down_at = down_at + widths[j]
    total = down_at
    up_at = jnp.int32(0)
    for j in range(n):
        held[asc + j] = up_at
        up_at = up_at + widths[j]

    def group(o, p):
        count = counts_ref[o]

        def one(j, c):
            b = order_ref[p + j]
            r = held[rank + j]
            held[rank + j] = r + 1
            head = j == 0
            u = held[desc + j] + r
            tab[jnp.where(head, plan.spare, plan.up + u)] = b
            tab[jnp.where(head, plan.spare, plan.up + u + total)] = b
            v = held[asc + j] + r
            tab[jnp.where(head, plan.spare, plan.down + v)] = b
            tab[jnp.where(head, plan.spare, plan.down + v + total)] = b
            tab[jnp.where(head, plan.first + o, plan.spare)] = b
            tab[plan.where + b] = held[base + j] + r
            mine = j == me
            tab[jnp.where(mine, plan.rank + o, plan.spare)] = r
            tab[jnp.where(mine, plan.slot + r, plan.spare)] = o
            return c

        lax.fori_loop(0, count, one, 0)
        return p + count

    lax.fori_loop(0, g, group, jnp.int32(0))
    s = plan.scalars
    tab[s + 0] = held[desc + prev]
    tab[s + 1] = held[width + prev]
    tab[s + 2] = total - held[width + prev] - held[width + me]
    tab[s + 3] = held[asc + nxt]
    tab[s + 4] = held[width + nxt]
    tab[s + 5] = total - held[width + nxt] - held[width + me]
    tab[s + 6] = jnp.where(counts_ref[col] > me, 1, 0)


def step_kernel(
    plan,
    grads, left, right, momentum, tab,
    update, new_momentum,
    gp, gm, landp, landm, outp, outm, zp, zm, abuf, gblk,
    lv, rv, mv, inner, outer, nm, ubuf, cbuf, fbuf,
    sq_own, sq_mid, sqz, sqs,
    load_sem, ring_send, ring_recv, z_send, zp_recv, zm_recv, a_send, a_recv,
    q_send, q_recv, u_send, u_recv, f_send, f_recv,
    *rbufs,
):
    n, g, nb = plan.planes, plan.groups, plan.blocks
    rows, cols = plan.rows, plan.cols
    slab = rows // g
    half = slab // 2
    width = cols // n
    me, col = lax.axis_index("dp"), lax.axis_index("shard")
    ahead, behind = lax.rem(me + 1, n), lax.rem(me + n - 1, n)

    def loop(low, high, body):
        lax.fori_loop(low, high, lambda i, c: (body(i), c)[1], 0)

    def remote(src, dst, send, recv, dp, shard):
        return pltpu.make_async_remote_copy(
            src_ref=src, dst_ref=dst, send_sem=send, recv_sem=recv,
            device_id={"dp": dp, "shard": shard}, device_id_type=MESH,
        )

    load_p = pltpu.make_async_copy(grads.at[0, :, 0:half, :], gp.at[0:nb], load_sem.at[0])
    load_m = pltpu.make_async_copy(grads.at[0, :, half:slab, :], gm.at[0:nb], load_sem.at[1])
    load_p.start()
    load_m.start()
    loads = [
        pltpu.make_async_copy(src.at[0], dst, load_sem.at[2 + i])
        for i, (src, dst) in enumerate(((left, lv), (right, rv), (momentum, mv)))
    ]

    barrier = pltpu.get_barrier_semaphore()
    for a in range(1, n):
        pl.semaphore_signal(
            barrier, inc=1, device_id={"dp": lax.rem(me + a, n), "shard": col}, device_id_type=MESH
        )

    def greet(a):
        pl.semaphore_signal(
            barrier, inc=1, device_id={"dp": me, "shard": lax.rem(col + a, g)}, device_id_type=MESH
        )

    loop(1, g, greet)
    pl.semaphore_wait(barrier, n - 1 + g - 1)
    load_p.wait()
    load_m.wait()
    for load in loads:
        load.start()

    sc = plan.scalars
    ways = (
        (gp, landp, outp, 0, ahead, plan.up + tab[sc], tab[sc + 1]),
        (gm, landm, outm, 1, behind, plan.down + tab[sc + 3], tab[sc + 4]),
    )

    def passing(way, k):
        _, land, out, d, to, _, _ = way
        return remote(out.at[k], land.at[k], ring_send.at[d], ring_recv.at[d, k], to, col)

    def take(k):
        for way in ways:
            held, land, _, _, _, start, lag = way
            passing(way, k).wait_recv()
            own = held[tab[start + lag + k]]
            held[nb + k] = (land[k].astype(F32) + own.astype(F32)).astype(BF16)

    def give(k):
        for way in ways:
            held, _, out, _, _, start, lag = way
            source = jnp.where(k < lag, tab[start + k], nb + k - lag)
            out[k] = held[source]
            passing(way, k).start()

    loop(0, LAG, give)

    def both(k):
        take(k - LAG)
        give(k)

    loop(LAG, plan.sends, both)
    loop(plan.sends - LAG, plan.sends, take)

    def exchange(t):
        @pl.when(t == 0)
        def _():
            gblk[pl.ds(col * slab, slab), :] = abuf[0]

        @pl.when(t > 0)
        def _():
            remote(
                abuf.at[t], gblk.at[pl.ds(col * slab, slab), :], a_send, a_recv,
                me, lax.rem(t + col, g),
            ).start()

    far = SKEW * (n - 1)
    lines = (
        (gp, zp, 0, zp_recv, ahead, me - 1, 1),
        (gm, zm, 1, zm_recv, behind, n - 1 - me, n - 1),
    )

    def along(line, q):
        _, zbuf, d, recv, to, _, _ = line
        return remote(zbuf.at[q], zbuf.at[q], z_send.at[d], recv.at[q], to, col)

    def first_block(line, q):
        return line[0][tab[plan.first + lax.rem(q + col, g)]].astype(F32)

    def chain(t):
        @pl.when(me != 0)
        def _():
            for line in lines:
                zbuf, hops, source = line[1], line[5], line[6]
                q = t - SKEW * hops

                @pl.when((q >= 0) & (q < g))
                def _():
                    @pl.when(me == source)
                    def _():
                        zbuf[q] = first_block(line, q).astype(BF16)

                    @pl.when(me != source)
                    def _():
                        along(line, q).wait_recv()
                        zbuf[q] = (zbuf[q].astype(F32) + first_block(line, q)).astype(BF16)

                    along(line, q).start()

            @pl.when(t < g)
            def _():
                r = tab[plan.rank + lax.rem(t + col, g)]
                abuf[t, 0:half, :] = gp[nb + tab[sc + 2] + r]
                abuf[t, half:slab, :] = gm[nb + tab[sc + 5] + r]
                exchange(t)

        @pl.when((me == 0) & (t >= far))
        def _():
            q = t - far
            for line, low in zip(lines, (0, half)):
                along(line, q).wait_recv()
                abuf[q, low:low + half, :] = (
                    line[1][q].astype(F32) + first_block(line, q)
                ).astype(BF16)
            exchange(q)

    loop(0, g + far, chain)

    remote(
        gblk.at[0:(g - 1) * slab], gblk.at[0:(g - 1) * slab], a_send, a_recv, me, col
    ).wait_recv()
    filled = tab[sc + 6] > 0
    tile = min(128, rows)

    def square(i, acc):
        x = gblk[pl.ds(pl.multiple_of(i * tile, tile), tile), :].astype(F32)
        return acc + jnp.sum(x * x, axis=0, keepdims=True)

    grad_square = jnp.sum(lax.fori_loop(0, rows // tile, square, jnp.zeros((1, cols), F32)))
    own_tile = jnp.full((8, 128), grad_square, F32)
    sq_own[...] = jnp.where(filled, own_tile, 0.0)
    sqz[me] = sq_own[...]
    for a in range(1, n):
        to = lax.rem(me + a, n)
        remote(sq_own, sqz.at[me], q_send.at[0], q_recv.at[0], to, col).start()
    for load in loads:
        load.wait()
    strip = 256

    def first_product(i, c):
        at = pl.ds(pl.multiple_of(i * strip, strip), strip)
        inner[:, at] = jnp.dot(lv[...], gblk[:, at], preferred_element_type=F32).astype(BF16)
        return c

    lax.fori_loop(0, cols // strip, first_product, 0)
    remote(sqz.at[0:n - 1], sqz.at[0:n - 1], q_send.at[0], q_recv.at[0], me, col).wait_recv()
    mid = sqz[0]
    for j in range(1, n):
        mid = mid + sqz[j]
    sq_mid[...] = mid
    sqs[col] = mid

    def tell(a):
        remote(
            sq_mid, sqs.at[col], q_send.at[1], q_recv.at[1], me, lax.rem(col + a, g)
        ).start()

    loop(1, g, tell)

    def second_product(i, acc):
        at = pl.ds(pl.multiple_of(i * strip, strip), strip)
        x = jnp.dot(inner[...], rv[:, at], preferred_element_type=F32)
        outer[:, at] = x
        return acc + jnp.sum(x * x, axis=0, keepdims=True)

    outer_square = jnp.sum(
        lax.fori_loop(0, cols // strip, second_product, jnp.zeros((1, strip), F32))
    )
    remote(sqs.at[0:g - 1], sqs.at[0:g - 1], q_send.at[1], q_recv.at[1], me, col).wait_recv()
    total = lax.fori_loop(0, g, lambda j, acc: acc + sqs[j], jnp.zeros((8, 128), F32))
    cells = float(rows * cols)
    outer_tile = jnp.full((8, 128), outer_square, F32)
    graft = (jnp.sqrt(own_tile / cells) * lax.rsqrt(outer_tile / cells + 1e-06))[0:1, :]
    clip = jnp.minimum(1.0, 0.5 * lax.rsqrt(total / (nb * cells) + 1e-06))[0:1, :]

    pairs = [(n // 2, 0)] + [(n // 2 - i, n // 2 + i) for i in range(1, n // 2)]
    for q, pair in enumerate(pairs):
        def part(i):
            at = pl.ds(pl.multiple_of(i * tile, tile), tile)
            for h, a in enumerate(pair):
                lanes = pl.ds(pl.multiple_of(lax.rem(me + a, n) * width, width), width)
                direction = jnp.where(filled, clip * (graft * outer[at, lanes]), 0.0)
                following = 0.9 * mv[at, lanes].astype(F32) + direction
                nm[at, lanes] = following.astype(BF16)
                ubuf[q, at, h * width:(h + 1) * width] = (
                    -0.8 * (0.9 * following + direction)
                ).astype(BF16)

        loop(0, rows // tile, part)
        rbufs[q][col] = ubuf[q, pl.ds(col * slab, slab), :]

        def back(a):
            to = lax.rem(col + a, g)
            remote(
                ubuf.at[q, pl.ds(to * slab, slab), :], rbufs[q].at[col],
                u_send.at[q], u_recv.at[q], me, to,
            ).start()

        loop(1, g, back)

    store = pltpu.make_async_copy(nm, new_momentum.at[0], load_sem.at[5])
    store.start()

    def home(q, h, j, to):
        return remote(
            cbuf.at[2 * q + h, 0:plan.most[j]], fbuf.at[plan.base[j]:plan.base[j] + plan.most[j]],
            f_send.at[2 * q + h], f_recv.at[j], to, col,
        )

    for q, pair in enumerate(pairs):
        remote(
            rbufs[q].at[0:g - 1], rbufs[q].at[0:g - 1], u_send.at[q], u_recv.at[q], me, col
        ).wait_recv()

        def gather(r):
            piece = rbufs[q][tab[plan.slot + r]]
            cbuf[2 * q, r] = piece[:, 0:width]
            cbuf[2 * q + 1, r] = piece[:, width:2 * width]

        loop(0, g, gather)
        for j in range(n):
            @pl.when(me == j)
            def _():
                for h, a in enumerate(pair):
                    if a == 0:
                        fbuf[plan.base[j]:plan.base[j] + plan.most[j]] = (
                            cbuf[2 * q + h, 0:plan.most[j]]
                        )
                    else:
                        home(q, h, j, lax.rem(me + a, n)).start()

    for j in range(n):
        @pl.when(me != j)
        def _():
            home(0, 0, j, me).wait_recv()

    def place(b):
        update[b] = fbuf[tab[plan.where + b]]

    loop(0, nb, place)
    store.wait()
    for way in ways:
        remote(way[2], way[1], ring_send.at[way[3]], ring_recv.at[0, 0], me, col).wait_send()

    @pl.when(me != 0)
    def _():
        for line in lines:
            remote(line[1], line[1], z_send.at[line[2]], line[3].at[0], me, col).wait_send()

    remote(abuf.at[1:g], abuf.at[1:g], a_send, a_recv, me, col).wait_send()
    remote(sqz.at[0:n - 1], sqz.at[0:n - 1], q_send.at[0], q_recv.at[0], me, col).wait_send()
    remote(sqs.at[0:g - 1], sqs.at[0:g - 1], q_send.at[1], q_recv.at[1], me, col).wait_send()
    for q, pair in enumerate(pairs):
        remote(
            rbufs[q].at[0:g - 1], rbufs[q].at[0:g - 1], u_send.at[q], u_recv.at[q], me, col
        ).wait_send()
        for j in range(n):
            @pl.when(me == j)
            def _():
                for h, a in enumerate(pair):
                    if a != 0:
                        home(q, h, j, me).wait_send()


def per_device(planes, groups, grads, left, right, momentum, block_order, owner_counts):
    blocks, slab, cols = grads.shape[1:]
    rows = left.shape[1]
    plan = Plan(planes, groups, blocks, rows, cols)
    half, width = slab // 2, cols // planes
    smem = pl.BlockSpec(memory_space=pltpu.SMEM)
    table = pl.pallas_call(
        functools.partial(table_kernel, plan),
        out_shape=jax.ShapeDtypeStruct((plan.size,), jnp.int32),
        in_specs=[smem, smem],
        out_specs=smem,
        scratch_shapes=[pltpu.SMEM((96,), jnp.int32)],
    )(block_order, owner_counts)
    anywhere = pl.BlockSpec(memory_space=pl.ANY)
    dma = pltpu.SemaphoreType.DMA
    held = plan.blocks + plan.sends
    return pl.pallas_call(
        functools.partial(step_kernel, plan),
        out_shape=(
            jax.ShapeDtypeStruct((blocks, slab, width), BF16),
            jax.ShapeDtypeStruct((1, rows, cols), BF16),
        ),
        in_specs=[anywhere] * 4 + [smem],
        out_specs=(pl.BlockSpec(memory_space=pltpu.VMEM), anywhere),
        scratch_shapes=(
            [pltpu.VMEM((held, half, cols), BF16)] * 2
            + [pltpu.VMEM((plan.sends, half, cols), BF16)] * 4
            + [pltpu.VMEM((groups, half, cols), BF16)] * 2
            + [pltpu.VMEM((groups, slab, cols), BF16), pltpu.VMEM((rows, cols), BF16)]
            + [
                pltpu.VMEM((rows, rows), BF16),
                pltpu.VMEM((cols, cols), BF16),
                pltpu.VMEM((rows, cols), BF16),
                pltpu.VMEM((rows, cols), BF16),
                pltpu.VMEM((rows, cols), F32),
                pltpu.VMEM((rows, cols), BF16),
                pltpu.VMEM((planes // 2, rows, 2 * width), BF16),
                pltpu.VMEM((planes, groups, slab, width), BF16),
                pltpu.VMEM((plan.slots, slab, width), BF16),
                pltpu.VMEM((8, 128), F32),
                pltpu.VMEM((8, 128), F32),
                pltpu.VMEM((planes, 8, 128), F32),
                pltpu.VMEM((groups, 8, 128), F32),
            ]
            + [
                dma((6,)),
                dma((2,)),
                dma((2, plan.sends)),
                dma((2,)),
                dma((groups,)),
                dma((groups,)),
                dma,
                dma,
                dma((2,)),
                dma((2,)),
                dma((planes // 2,)),
                dma((planes // 2,)),
                dma((planes,)),
                dma((planes,)),
            ]
            + [pltpu.VMEM((groups, slab, 2 * width), BF16)] * (planes // 2)
        ),
        compiler_params=pltpu.CompilerParams(
            collective_id=0, has_side_effects=True, vmem_limit_bytes=56 * 1024 * 1024
        ),
        cost_estimate=pl.CostEstimate(
            flops=2 * rows * cols * (rows + cols), bytes_accessed=2 * 13 * rows * cols // 2,
            transcendentals=0,
        ),
    )(grads, left, right, momentum, table)


def solution(mesh):
    slots = P(("dp", "shard"), None, None)
    return jax.shard_map(
        functools.partial(per_device, mesh.shape["dp"], mesh.shape["shard"]),
        mesh=mesh,
        in_specs=(P("dp", None, "shard", None), slots, slots, slots, P(), P()),
        out_specs=(P(None, "shard", "dp"), slots),
        check_vma=False,
    )
```

time: 438 us -> 185 us (0.42)
  blocking collectives: 199 us -> 0 us
  Pallas kernels: 0 us -> 180 us
  waiting for transfers between devices: 84.9 us -> 0 us
  local copies, waits for them, and re-layouts: 84.4 us -> 4.95 us
  other arithmetic: 27.3 us -> 0 us
  between operations: 16.3 us -> 0.65 us
  starting transfers between devices: 14.9 us -> 0 us
  matrix products: 9.43 us -> 0 us
    pallas_call x0 -> x2, Pallas kernels: none -> 180 us  [the longest x1 174 us: per_device(): pl.pallas_call(functools.partial(step_kernel, plan), out_shape=(jax.Shape...]
    all_to_all x2 -> x0, blocking collectives: 107 us -> none  [the longest x1 53.7 us: per_device(): lax.all_to_all(outgoing, 'dp', split_axis=1, concat_axis=3, tiled=True)]
    psum x1 -> x0, blocking collectives: 92.1 us -> none  [per_device(): grand_total = lax.psum(jnp.sum(widened * widened), ('dp', 'shard'))]
    unnamed x16 -> x2, local copies, waits for them, and re-layouts: 64.9 us -> 4.95 us
    unnamed x2 -> x0, waiting for transfers between devices: 57.3 us -> none
    all_to_all x2 -> x0, waiting for transfers between devices: 27.6 us -> none  [the longest x1 27.6 us: per_device(): lax.all_to_all(lax.all_to_all(sending, 'dp', split_axis=3, concat_axis=1,...]
    all_to_all x2 -> x0, starting transfers between devices: 14.9 us -> none  [the longest x1 9.26 us: per_device(): lax.all_to_all(lax.all_to_all(outgoing, 'dp', split_axis=1, concat_axis=3...]
    unnamed x1 -> x0, other arithmetic: 12.8 us -> none
  transfers between devices with their start and end apart: 3 -> 0, of which waited for: 2 -> 0; matrix products, arithmetic and copies ran while one was open for 1% -> 0% of each run, Pallas kernels for 0% -> 0%
where the time goes in v1:
time: 185 us
  Pallas kernels  180 us (97%)
  local copies, waits for them, and re-layouts  4.95 us (3%)
    pallas_call x1, Pallas kernels, per_device(): pl.pallas_call(functools.partial(step_kernel, plan), out_shape=(jax.Shape...  174 us
    pallas_call x1, Pallas kernels, per_device(): pl.pallas_call(functools.partial(table_kernel, plan), out_shape=jax.Shape...  5.49 us
    unnamed x2, local copies, waits for them, and re-layouts  4.95 us

profile of v1, /device:TPU:1, one launch (start us, length us, event | category | flops | bytes accessed | tf_op | source)
XLA Modules:
  0.0 185.3 jit_solution(9959717566345439942)
XLA Ops:
  0.6 5.5 %shard_map.77.tab = s32[393]{0:T(512)} custom-call(s32[64]{0:T(128)} %order_ref.1, s32[32]{0:T(128)} %counts_ref.1), custom_call_target="tpu_custom_call" | custom-call | tf_op jit(solution)/shard_map/pallas_call | solution.py:421
  6.1 174.2 %shard_map.78 = (bf16[64,32,128]{2,1,0:T(8,128)(2,1)}, bf16[1,1024,1024]{2,1,0:T(8,128)(2,1)}) custom-call(bf16[1,64,32,1024]{3,2,1,0:T(8,128)(2,1)} %grads.1, bf16[1,1024,1024]{2,1,0:T(8,128)(2,1)} %left.1, bf16[1,1024,1024]{2,1,0:T(8,128)(2,1)} %right.1, bf16[1,1024,1024]{2,1,0:T(8,128)(2,1)} %momentum.1, s32[393]{0:T(512)} %shard_map.77.tab), custom_call_target="tpu_custom_call" | custom-call | flops 4294967296 | bytes 13631488 | tf_op jit(solution)/shard_map/pallas_call | solution.py:431
  180.3 1.9 %copy.10 = bf16[64,32,128]{2,1,0:T(8,128)(2,1)} copy(bf16[64,32,128]{2,1,0:T(8,128)(2,1)} %get-tuple-element.4) | data formatting | bytes 1048576
  182.2 3.1 %copy.11 = bf16[1,1024,1024]{2,1,0:T(8,128)(2,1)} copy(bf16[1,1024,1024]{2,1,0:T(8,128)(2,1)} %get-tuple-element.5) | data formatting | bytes 4194304

commit v2 on v1

--- a/solution.py
+++ b/solution.py
@@ -8,8 +8,9 @@
 from jax.sharding import PartitionSpec as P
 
 MESH = pl.DeviceIdType.MESH
-LAG = 4
+LAG = 2
 SKEW = 3
+EARLY = 9
 F32 = jnp.float32
 BF16 = jnp.bfloat16
 
@@ -25,16 +26,14 @@
         self.base = [sum(self.most[:j]) for j in range(planes)]
         self.slots = sum(self.most)
         self.sends = max(extras - (planes - 2), LAG) + (planes - 2) * LAG
-        self.listed = 2 * (self.sends + LAG)
         place = 0
         for name, size in (
-            ("up", self.listed),
-            ("down", self.listed),
+            ("before", self.sends),
+            ("order", 2 * (self.sends + LAG)),
             ("first", groups),
             ("rank", groups),
             ("slot", groups),
             ("where", blocks),
-            ("spare", 1),
             ("scalars", 16),
         ):
             setattr(self, name, place)
@@ -46,38 +45,39 @@
     n, g = plan.planes, plan.groups
     me, col = lax.axis_index("dp"), lax.axis_index("shard")
     prev, nxt = lax.rem(me + n - 1, n), lax.rem(me + 1, n)
-
-    def clear(i, c):
+    hist, start, rank, width = 0, 16, 32, 48
+    for i in range(plan.first):
         tab[i] = 0
-        return c
-
-    lax.fori_loop(0, plan.size, clear, 0)
-    hist, desc, asc, rank, base, width = 0, 16, 32, 48, 64, 80
     for i in range(16):
         held[hist + i] = 0
         held[rank + i] = 0
 
-    def tally(o, c):
+    def tally(o, seen):
+        p, mine = seen
         k = counts_ref[o]
         held[hist + k] = held[hist + k] + 1
-        return c
-
-    lax.fori_loop(0, g, tally, 0)
+        b = order_ref[p]
+        tab[plan.first + o] = b
+        tab[plan.where + b] = o
+        tab[plan.rank + o] = jnp.where(k > me, mine, 0)
+        tab[plan.slot + o] = 0
+        tab[plan.slot + mine] = o
+        return p + k, mine + jnp.where(k > me, 1, 0)
+
+    lax.fori_loop(0, g, tally, (jnp.int32(0), jnp.int32(0)))
     run = jnp.int32(0)
-    down_at = jnp.int32(0)
-    widths = [None] * n
+    at = jnp.int32(0)
     for j in range(n - 1, -1, -1):
         run = run + held[hist + j + 1]
-        widths[j] = jnp.int32(LAG) if j == 0 else jnp.maximum(run, LAG)
-        held[desc + j] = down_at
-        held[width + j] = widths[j]
-        held[base + j] = plan.base[j]
-        down_at = down_at + widths[j]
-    total = down_at
-    up_at = jnp.int32(0)
-    for j in range(n):
-        held[asc + j] = up_at
-        up_at = up_at + widths[j]
+        wide = jnp.int32(LAG) if j == 0 else jnp.maximum(run, LAG)
+        held[start + j] = at
+        held[width + j] = wide
+        at = at + wide
+    total = at
+    for r in range(LAG):
+        b = tab[plan.first + lax.rem(col + r, g)]
+        tab[plan.order + held[start] + r] = b
+        tab[plan.order + held[start] + r + total] = b
 
     def group(o, p):
         count = counts_ref[o]
@@ -86,38 +86,34 @@
             b = order_ref[p + j]
             r = held[rank + j]
             held[rank + j] = r + 1
-            head = j == 0
-            u = held[desc + j] + r
-            tab[jnp.where(head, plan.spare, plan.up + u)] = b
-            tab[jnp.where(head, plan.spare, plan.up + u + total)] = b
-            v = held[asc + j] + r
-            tab[jnp.where(head, plan.spare, plan.down + v)] = b
-            tab[jnp.where(head, plan.spare, plan.down + v + total)] = b
-            tab[jnp.where(head, plan.first + o, plan.spare)] = b
-            tab[plan.where + b] = held[base + j] + r
-            mine = j == me
-            tab[jnp.where(mine, plan.rank + o, plan.spare)] = r
-            tab[jnp.where(mine, plan.slot + r, plan.spare)] = o
+            u = plan.order + held[start + j] + r
+            tab[u] = b
+            tab[u + total] = b
+            offset = jnp.int32(plan.base[1])
+            for i in range(2, n):
+                offset = jnp.where(j >= i, plan.base[i], offset)
+            tab[plan.where + b] = offset + r
             return c
 
-        lax.fori_loop(0, count, one, 0)
+        lax.fori_loop(1, count, one, 0)
         return p + count
 
     lax.fori_loop(0, g, group, jnp.int32(0))
     s = plan.scalars
-    tab[s + 0] = held[desc + prev]
-    tab[s + 1] = held[width + prev]
-    tab[s + 2] = total - held[width + prev] - held[width + me]
-    tab[s + 3] = held[asc + nxt]
-    tab[s + 4] = held[width + nxt]
-    tab[s + 5] = total - held[width + nxt] - held[width + me]
+    before, after, own = held[width + prev], held[width + nxt], held[width + me]
+    tab[s + 0] = plan.order + held[start + prev]
+    tab[s + 1] = before
+    tab[s + 2] = total - before - own
+    tab[s + 3] = plan.order + held[start + nxt] + after - 1 + total
+    tab[s + 4] = after
+    tab[s + 5] = total - after - 1
     tab[s + 6] = jnp.where(counts_ref[col] > me, 1, 0)
 
 
 def step_kernel(
     plan,
     grads, left, right, momentum, tab,
-    update, new_momentum,
+    pieces, new_momentum,
     gp, gm, landp, landm, outp, outm, zp, zm, abuf, gblk,
     lv, rv, mv, inner, outer, nm, ubuf, cbuf, fbuf,
     sq_own, sq_mid, sqz, sqs,
@@ -171,36 +167,40 @@
 
     sc = plan.scalars
     ways = (
-        (gp, landp, outp, 0, ahead, plan.up + tab[sc], tab[sc + 1]),
-        (gm, landm, outm, 1, behind, plan.down + tab[sc + 3], tab[sc + 4]),
+        (gp, landp, outp, 0, ahead, tab[sc], 1, tab[sc + 1]),
+        (gm, landm, outm, 1, behind, tab[sc + 3], -1, tab[sc + 4]),
     )
-
-    def passing(way, k):
-        _, land, out, d, to, _, _ = way
-        return remote(out.at[k], land.at[k], ring_send.at[d], ring_recv.at[d, k], to, col)
-
-    def take(k):
+    parts = tuple(slice(h * (cols // 2), (h + 1) * (cols // 2)) for h in range(2))
+
+    def passing(way, k, h):
+        _, land, out, d, to, _, _, _ = way
+        return remote(
+            out.at[k, :, parts[h]], land.at[k, :, parts[h]],
+            ring_send.at[d], ring_recv.at[2 * d + h, k], to, col,
+        )
+
+    def take(k, h):
         for way in ways:
-            held, land, _, _, _, start, lag = way
-            passing(way, k).wait_recv()
-            own = held[tab[start + lag + k]]
-            held[nb + k] = (land[k].astype(F32) + own.astype(F32)).astype(BF16)
-
-    def give(k):
+            held, land, _, _, _, start, sign, lag = way
+            passing(way, k, h).wait_recv()
+            own = held[tab[jnp.maximum(start + sign * (lag + k), 0)], :, parts[h]]
+            held[nb + k, :, parts[h]] = (
+                land[k, :, parts[h]].astype(F32) + own.astype(F32)
+            ).astype(BF16)
+
+    def give(k, h):
         for way in ways:
-            held, _, out, _, _, start, lag = way
-            source = jnp.where(k < lag, tab[start + k], nb + k - lag)
-            out[k] = held[source]
-            passing(way, k).start()
-
-    loop(0, LAG, give)
-
-    def both(k):
-        take(k - LAG)
-        give(k)
-
-    loop(LAG, plan.sends, both)
-    loop(plan.sends - LAG, plan.sends, take)
+            held, _, out, _, _, start, sign, lag = way
+            source = jnp.where(k < lag, tab[jnp.maximum(start + sign * k, 0)], nb + k - lag)
+            out[k, :, parts[h]] = held[source, :, parts[h]]
+            passing(way, k, h).start()
+
+    def ring(k, taking=True, giving=True):
+        for h in range(2):
+            if taking:
+                take(k - LAG, h)
+            if giving:
+                give(k, h)
 
     def exchange(t):
         @pl.when(t == 0)
@@ -219,6 +219,8 @@
         (gp, zp, 0, zp_recv, ahead, me - 1, 1),
         (gm, zm, 1, zm_recv, behind, n - 1 - me, n - 1),
     )
+    begin, ready = max(plan.sends - EARLY, LAG), plan.sends + LAG
+    end = max(begin + far + g - LAG, ready + g)
 
     def along(line, q):
         _, zbuf, d, recv, to, _, _ = line
@@ -232,9 +234,9 @@
         def _():
             for line in lines:
                 zbuf, hops, source = line[1], line[5], line[6]
-                q = t - SKEW * hops
-
-                @pl.when((q >= 0) & (q < g))
+                q = t - begin - SKEW * hops + LAG
+
+                @pl.when((q >= LAG) & (q < g))
                 def _():
                     @pl.when(me == source)
                     def _():
@@ -247,16 +249,9 @@
 
                     along(line, q).start()
 
-            @pl.when(t < g)
-            def _():
-                r = tab[plan.rank + lax.rem(t + col, g)]
-                abuf[t, 0:half, :] = gp[nb + tab[sc + 2] + r]
-                abuf[t, half:slab, :] = gm[nb + tab[sc + 5] + r]
-                exchange(t)
-
-        @pl.when((me == 0) & (t >= far))
+        @pl.when((me == 0) & (t >= begin + far) & (t < begin + far + g - LAG))
         def _():
-            q = t - far
+            q = t - begin - far + LAG
             for line, low in zip(lines, (0, half)):
                 along(line, q).wait_recv()
                 abuf[q, low:low + half, :] = (
@@ -264,7 +259,21 @@
                 ).astype(BF16)
             exchange(q)
 
-    loop(0, g + far, chain)
+    def settle(t):
+        i = t - ready
+
+        @pl.when((i < g) & ((me != 0) | (i < LAG)))
+        def _():
+            r = jnp.where(me == 0, i, tab[plan.rank + lax.rem(i + col, g)])
+            abuf[i, 0:half, :] = gp[nb + tab[sc + 2] + r]
+            abuf[i, half:slab, :] = gm[nb + tab[sc + 5] - r]
+            exchange(i)
+
+    loop(0, LAG, lambda k: ring(k, taking=False))
+    loop(LAG, begin, ring)
+    loop(begin, plan.sends, lambda k: (ring(k), chain(k)))
+    loop(plan.sends, ready, lambda k: (ring(k, giving=False), chain(k)))
+    loop(ready, end, lambda k: (chain(k), settle(k)))
 
     remote(
         gblk.at[0:(g - 1) * slab], gblk.at[0:(g - 1) * slab], a_send, a_recv, me, col
@@ -324,7 +333,13 @@
     clip = jnp.minimum(1.0, 0.5 * lax.rsqrt(total / (nb * cells) + 1e-06))[0:1, :]
 
     pairs = [(n // 2, 0)] + [(n // 2 - i, n // 2 + i) for i in range(1, n // 2)]
-    for q, pair in enumerate(pairs):
+    def home(q, h, j, to):
+        return remote(
+            cbuf.at[2 * q + h, 0:plan.most[j]], fbuf.at[plan.base[j]:plan.base[j] + plan.most[j]],
+            f_send.at[2 * q + h], f_recv.at[j], to, col,
+        )
+
+    def outward(q, pair):
         def part(i):
             at = pl.ds(pl.multiple_of(i * tile, tile), tile)
             for h, a in enumerate(pair):
@@ -348,16 +363,7 @@
 
         loop(1, g, back)
 
-    store = pltpu.make_async_copy(nm, new_momentum.at[0], load_sem.at[5])
-    store.start()
-
-    def home(q, h, j, to):
-        return remote(
-            cbuf.at[2 * q + h, 0:plan.most[j]], fbuf.at[plan.base[j]:plan.base[j] + plan.most[j]],
-            f_send.at[2 * q + h], f_recv.at[j], to, col,
-        )
-
-    for q, pair in enumerate(pairs):
+    def homeward(q, pair):
         remote(
             rbufs[q].at[0:g - 1], rbufs[q].at[0:g - 1], u_send.at[q], u_recv.at[q], me, col
         ).wait_recv()
@@ -379,23 +385,32 @@
                     else:
                         home(q, h, j, lax.rem(me + a, n)).start()
 
+    for q, pair in enumerate(pairs):
+        outward(q, pair)
+        if q > 0:
+            homeward(q - 1, pairs[q - 1])
+    store = pltpu.make_async_copy(nm, new_momentum.at[0], load_sem.at[5])
+    store.start()
+    homeward(len(pairs) - 1, pairs[-1])
+
     for j in range(n):
         @pl.when(me != j)
         def _():
             home(0, 0, j, me).wait_recv()
 
-    def place(b):
-        update[b] = fbuf[tab[plan.where + b]]
-
-    loop(0, nb, place)
+    keep = pltpu.make_async_copy(fbuf, pieces, load_sem.at[0])
+    keep.start()
     store.wait()
+    keep.wait()
     for way in ways:
         remote(way[2], way[1], ring_send.at[way[3]], ring_recv.at[0, 0], me, col).wait_send()
 
     @pl.when(me != 0)
     def _():
         for line in lines:
-            remote(line[1], line[1], z_send.at[line[2]], line[3].at[0], me, col).wait_send()
+            remote(
+                line[1].at[LAG:g], line[1].at[LAG:g], z_send.at[line[2]], line[3].at[0], me, col
+            ).wait_send()
 
     remote(abuf.at[1:g], abuf.at[1:g], a_send, a_recv, me, col).wait_send()
     remote(sqz.at[0:n - 1], sqz.at[0:n - 1], q_send.at[0], q_recv.at[0], me, col).wait_send()
@@ -412,6 +427,27 @@
                         home(q, h, j, me).wait_send()
 
 
+def last_kernel(plan, pieces, following, tab, update, new_momentum, sems):
+    step = plan.rows // 4
+    copies = [
+        pltpu.make_async_copy(
+            following.at[0, i * step:(i + 1) * step], new_momentum.at[0, i * step:(i + 1) * step],
+            sems.at[i],
+        )
+        for i in range(4)
+    ]
+    for copy in copies:
+        copy.start()
+
+    def place(b, c):
+        update[b] = pieces[tab[plan.where + b]]
+        return c
+
+    lax.fori_loop(0, plan.blocks, place, 0)
+    for copy in copies:
+        copy.wait()
+
+
 def per_device(planes, groups, grads, left, right, momentum, block_order, owner_counts):
     blocks, slab, cols = grads.shape[1:]
     rows = left.shape[1]
@@ -423,19 +459,19 @@
         out_shape=jax.ShapeDtypeStruct((plan.size,), jnp.int32),
         in_specs=[smem, smem],
         out_specs=smem,
-        scratch_shapes=[pltpu.SMEM((96,), jnp.int32)],
+        scratch_shapes=[pltpu.SMEM((64,), jnp.int32)],
     )(block_order, owner_counts)
     anywhere = pl.BlockSpec(memory_space=pl.ANY)
     dma = pltpu.SemaphoreType.DMA
     held = plan.blocks + plan.sends
-    return pl.pallas_call(
+    pieces, following = pl.pallas_call(
         functools.partial(step_kernel, plan),
         out_shape=(
-            jax.ShapeDtypeStruct((blocks, slab, width), BF16),
+            jax.ShapeDtypeStruct((plan.slots, slab, width), BF16),
             jax.ShapeDtypeStruct((1, rows, cols), BF16),
         ),
         in_specs=[anywhere] * 4 + [smem],
-        out_specs=(pl.BlockSpec(memory_space=pltpu.VMEM), anywhere),
+        out_specs=(anywhere, anywhere),
         scratch_shapes=(
             [pltpu.VMEM((held, half, cols), BF16)] * 2
             + [pltpu.VMEM((plan.sends, half, cols), BF16)] * 4
@@ -459,7 +495,7 @@
             + [
                 dma((6,)),
                 dma((2,)),
-                dma((2, plan.sends)),
+                dma((4, plan.sends)),
                 dma((2,)),
                 dma((groups,)),
                 dma((groups,)),
@@ -482,6 +518,16 @@
             transcendentals=0,
         ),
     )(grads, left, right, momentum, table)
+    return pl.pallas_call(
+        functools.partial(last_kernel, plan),
+        out_shape=(
+            jax.ShapeDtypeStruct((blocks, slab, width), BF16),
+            jax.ShapeDtypeStruct((1, rows, cols), BF16),
+        ),
+        in_specs=[pl.BlockSpec(memory_space=pltpu.VMEM), anywhere, smem],
+        out_specs=(pl.BlockSpec(memory_space=pltpu.VMEM), anywhere),
+        scratch_shapes=[dma((4,))],
+    )(pieces, following, table)
 
 
 def solution(mesh):

time: 185 us -> 250 us (1.35)
  Pallas kernels: 180 us -> 249 us
  local copies, waits for them, and re-layouts: 4.95 us -> 0 us
    pallas_call x0 -> x1, Pallas kernels: none -> 66.6 us  [per_device(): pl.pallas_call(functools.partial(last_kernel, plan), out_shape=(jax.Shape...]
    pallas_call x1, Pallas kernels: 174 us -> 180 us  [per_device(): pl.pallas_call(functools.partial(step_kernel, plan), out_shape=(jax.Shape...]
    unnamed x2 -> x0, local copies, waits for them, and re-layouts: 4.95 us -> none
    pallas_call x1, Pallas kernels: 5.49 us -> 2.57 us  [per_device(): pl.pallas_call(functools.partial(table_kernel, plan), out_shape=jax.Shape...]
where the time goes in v2:
time: 250 us
  Pallas kernels  249 us (100%)
    pallas_call x1, Pallas kernels, per_device(): pl.pallas_call(functools.partial(step_kernel, plan), out_shape=(jax.Shape...  180 us
    pallas_call x1, Pallas kernels, per_device(): pl.pallas_call(functools.partial(last_kernel, plan), out_shape=(jax.Shape...  66.6 us

profile of v2, /device:TPU:1, one launch (start us, length us, event | category | flops | bytes accessed | tf_op | source)
XLA Modules:
  0.0 250.0 jit_solution(17745785203152049611)
XLA Ops:
  0.6 2.6 %shard_map.77.tab = s32[294]{0:T(512)} custom-call(s32[64]{0:T(128)} %order_ref.1, s32[32]{0:T(128)} %counts_ref.1), custom_call_target="tpu_custom_call" | custom-call | tf_op jit(solution)/shard_map/pallas_call | solution.py:457
  3.2 180.2 %shard_map.78 = (bf16[102,32,128]{2,1,0:T(8,128)(2,1)}, bf16[1,1024,1024]{2,1,0:T(8,128)(2,1)}) custom-call(bf16[1,64,32,1024]{3,2,1,0:T(8,128)(2,1)} %grads.1, bf16[1,1024,1024]{2,1,0:T(8,128)(2,1)} %left.1, bf16[1,1024,1024]{2,1,0:T(8,128)(2,1)} %right.1, bf16[1,1024,1024]{2,1,0:T(8,128)(2,1)} %momentum.1, s32[294]{0:T(512)} %shard_map.77.tab), custom_call_target="tpu_custom_call" | custom-call | flops 4294967296 | bytes 13631488 | tf_op jit(solution)/shard_map/pallas_call | solution.py:467
  183.4 66.6 %shard_map.79 = (bf16[64,32,128]{2,1,0:T(8,128)(2,1)}, bf16[1,1024,1024]{2,1,0:T(8,128)(2,1)}) custom-call(bf16[102,32,128]{2,1,0:T(8,128)(2,1)} %get-tuple-element.4.pieces, bf16[1,1024,1024]{2,1,0:T(8,128)(2,1)} %get-tuple-element.5.following, s32[294]{0:T(512)} %shard_map.77.tab), custom_call_target="tpu_custom_call" | custom-call | tf_op jit(solution)/shard_map/pallas_call | solution.py:521

commit v3 on v2

--- a/solution.py
+++ b/solution.py
@@ -8,9 +8,10 @@
 from jax.sharding import PartitionSpec as P
 
 MESH = pl.DeviceIdType.MESH
-LAG = 2
-SKEW = 3
-EARLY = 9
+LAG = 4
+PARTS = 1
+SKEW = 4
+EARLY = 24
 F32 = jnp.float32
 BF16 = jnp.bfloat16
 
@@ -170,13 +171,13 @@
         (gp, landp, outp, 0, ahead, tab[sc], 1, tab[sc + 1]),
         (gm, landm, outm, 1, behind, tab[sc + 3], -1, tab[sc + 4]),
     )
-    parts = tuple(slice(h * (cols // 2), (h + 1) * (cols // 2)) for h in range(2))
+    parts = tuple(slice(h * (cols // PARTS), (h + 1) * (cols // PARTS)) for h in range(PARTS))
 
     def passing(way, k, h):
         _, land, out, d, to, _, _, _ = way
         return remote(
             out.at[k, :, parts[h]], land.at[k, :, parts[h]],
-            ring_send.at[d], ring_recv.at[2 * d + h, k], to, col,
+            ring_send.at[d], ring_recv.at[PARTS * d + h, k], to, col,
         )
 
     def take(k, h):
@@ -196,7 +197,7 @@
             passing(way, k, h).start()
 
     def ring(k, taking=True, giving=True):
-        for h in range(2):
+        for h in range(PARTS):
             if taking:
                 take(k - LAG, h)
             if giving:
@@ -427,25 +428,30 @@
                         home(q, h, j, me).wait_send()
 
 
-def last_kernel(plan, pieces, following, tab, update, new_momentum, sems):
+def last_kernel(plan, pieces, following, tab, update, new_momentum, through, sems):
     step = plan.rows // 4
-    copies = [
-        pltpu.make_async_copy(
-            following.at[0, i * step:(i + 1) * step], new_momentum.at[0, i * step:(i + 1) * step],
-            sems.at[i],
-        )
-        for i in range(4)
+    rows = [slice(i * step, (i + 1) * step) for i in range(4)]
+    reads = [
+        pltpu.make_async_copy(following.at[0, r], through.at[r], sems.at[i])
+        for i, r in enumerate(rows)
     ]
-    for copy in copies:
-        copy.start()
+    writes = [
+        pltpu.make_async_copy(through.at[r], new_momentum.at[0, r], sems.at[4 + i])
+        for i, r in enumerate(rows)
+    ]
+    for read in reads:
+        read.start()
 
     def place(b, c):
         update[b] = pieces[tab[plan.where + b]]
         return c
 
     lax.fori_loop(0, plan.blocks, place, 0)
-    for copy in copies:
-        copy.wait()
+    for read, write in zip(reads, writes):
+        read.wait()
+        write.start()
+    for write in writes:
+        write.wait()
 
 
 def per_device(planes, groups, grads, left, right, momentum, block_order, owner_counts):
@@ -495,7 +501,7 @@
             + [
                 dma((6,)),
                 dma((2,)),
-                dma((4, plan.sends)),
+                dma((2 * PARTS, plan.sends)),
                 dma((2,)),
                 dma((groups,)),
                 dma((groups,)),
@@ -526,7 +532,7 @@
         ),
         in_specs=[pl.BlockSpec(memory_space=pltpu.VMEM), anywhere, smem],
         out_specs=(pl.BlockSpec(memory_space=pltpu.VMEM), anywhere),
-        scratch_shapes=[dma((4,))],
+        scratch_shapes=[pltpu.VMEM((rows, cols), BF16), dma((8,))],
     )(pieces, following, table)
 
 

time: 250 us -> 165 us (0.66)
  Pallas kernels: 249 us -> 164 us
    pallas_call x1, Pallas kernels: 66.6 us -> 4.37 us  [per_device(): pl.pallas_call(functools.partial(last_kernel, plan), out_shape=(jax.Shape...]
    pallas_call x1, Pallas kernels: 180 us -> 157 us  [per_device(): pl.pallas_call(functools.partial(step_kernel, plan), out_shape=(jax.Shape...]
where the time goes in v3:
time: 165 us
  Pallas kernels  164 us (99%)
    pallas_call x1, Pallas kernels, per_device(): pl.pallas_call(functools.partial(step_kernel, plan), out_shape=(jax.Shape...  157 us
    pallas_call x1, Pallas kernels, per_device(): pl.pallas_call(functools.partial(last_kernel, plan), out_shape=(jax.Shape...  4.37 us

profile of v3, /device:TPU:1, one launch (start us, length us, event | category | flops | bytes accessed | tf_op | source)
XLA Modules:
  0.0 165.0 jit_solution(2978569172093805570)
XLA Ops:
  0.6 2.6 %shard_map.77.tab = s32[334]{0:T(512)} custom-call(s32[64]{0:T(128)} %order_ref.1, s32[32]{0:T(128)} %counts_ref.1), custom_call_target="tpu_custom_call" | custom-call | tf_op jit(solution)/shard_map/pallas_call | solution.py:463
  3.2 157.4 %shard_map.78 = (bf16[102,32,128]{2,1,0:T(8,128)(2,1)}, bf16[1,1024,1024]{2,1,0:T(8,128)(2,1)}) custom-call(bf16[1,64,32,1024]{3,2,1,0:T(8,128)(2,1)} %grads.1, bf16[1,1024,1024]{2,1,0:T(8,128)(2,1)} %left.1, bf16[1,1024,1024]{2,1,0:T(8,128)(2,1)} %right.1, bf16[1,1024,1024]{2,1,0:T(8,128)(2,1)} %momentum.1, s32[334]{0:T(512)} %shard_map.77.tab), custom_call_target="tpu_custom_call" | custom-call | flops 4294967296 | bytes 13631488 | tf_op jit(solution)/shard_map/pallas_call | solution.py:473
  160.6 4.4 %shard_map.79 = (bf16[64,32,128]{2,1,0:T(8,128)(2,1)}, bf16[1,1024,1024]{2,1,0:T(8,128)(2,1)}) custom-call(bf16[102,32,128]{2,1,0:T(8,128)(2,1)} %get-tuple-element.4.pieces, bf16[1,1024,1024]{2,1,0:T(8,128)(2,1)} %get-tuple-element.5.following, s32[334]{0:T(512)} %shard_map.77.tab), custom_call_target="tpu_custom_call" | custom-call | tf_op jit(solution)/shard_map/pallas_call | solution.py:527

commit v4 on v3

--- a/solution.py
+++ b/solution.py
@@ -8,10 +8,10 @@
 from jax.sharding import PartitionSpec as P
 
 MESH = pl.DeviceIdType.MESH
-LAG = 4
+LAG = 3
 PARTS = 1
 SKEW = 4
-EARLY = 24
+EARLY = 20
 F32 = jnp.float32
 BF16 = jnp.bfloat16
 
@@ -42,6 +42,10 @@
         self.size = place
 
 
+def chunks_of(n):
+    return [(n // 2,)] + [(n // 2 - i, n // 2 + i) for i in range(1, n // 2)] + [(0,)]
+
+
 def table_kernel(plan, order_ref, counts_ref, tab, held):
     n, g = plan.planes, plan.groups
     me, col = lax.axis_index("dp"), lax.axis_index("shard")
@@ -333,11 +337,11 @@
     graft = (jnp.sqrt(own_tile / cells) * lax.rsqrt(outer_tile / cells + 1e-06))[0:1, :]
     clip = jnp.minimum(1.0, 0.5 * lax.rsqrt(total / (nb * cells) + 1e-06))[0:1, :]
 
-    pairs = [(n // 2, 0)] + [(n // 2 - i, n // 2 + i) for i in range(1, n // 2)]
-    def home(q, h, j, to):
+    pairs = chunks_of(n)
+    def home(a, j, to):
         return remote(
-            cbuf.at[2 * q + h, 0:plan.most[j]], fbuf.at[plan.base[j]:plan.base[j] + plan.most[j]],
-            f_send.at[2 * q + h], f_recv.at[j], to, col,
+            cbuf.at[a, 0:plan.most[j]], fbuf.at[plan.base[j]:plan.base[j] + plan.most[j]],
+            f_send.at[a], f_recv.at[j], to, col,
         )
 
     def outward(q, pair):
@@ -353,12 +357,12 @@
                 ).astype(BF16)
 
         loop(0, rows // tile, part)
-        rbufs[q][col] = ubuf[q, pl.ds(col * slab, slab), :]
+        rbufs[q][col] = ubuf[q, pl.ds(col * slab, slab), 0:len(pair) * width]
 
         def back(a):
             to = lax.rem(col + a, g)
             remote(
-                ubuf.at[q, pl.ds(to * slab, slab), :], rbufs[q].at[col],
+                ubuf.at[q, pl.ds(to * slab, slab), 0:len(pair) * width], rbufs[q].at[col],
                 u_send.at[q], u_recv.at[q], me, to,
             ).start()
 
@@ -371,20 +375,20 @@
 
         def gather(r):
             piece = rbufs[q][tab[plan.slot + r]]
-            cbuf[2 * q, r] = piece[:, 0:width]
-            cbuf[2 * q + 1, r] = piece[:, width:2 * width]
+            for h, a in enumerate(pair):
+                cbuf[a, r] = piece[:, h * width:(h + 1) * width]
 
         loop(0, g, gather)
         for j in range(n):
             @pl.when(me == j)
             def _():
-                for h, a in enumerate(pair):
+                for a in pair:
                     if a == 0:
                         fbuf[plan.base[j]:plan.base[j] + plan.most[j]] = (
-                            cbuf[2 * q + h, 0:plan.most[j]]
+                            cbuf[a, 0:plan.most[j]]
                         )
                     else:
-                        home(q, h, j, lax.rem(me + a, n)).start()
+                        home(a, j, lax.rem(me + a, n)).start()
 
     for q, pair in enumerate(pairs):
         outward(q, pair)
@@ -397,7 +401,7 @@
     for j in range(n):
         @pl.when(me != j)
         def _():
-            home(0, 0, j, me).wait_recv()
+            home(0, j, me).wait_recv()
 
     keep = pltpu.make_async_copy(fbuf, pieces, load_sem.at[0])
     keep.start()
@@ -423,14 +427,15 @@
         for j in range(n):
             @pl.when(me == j)
             def _():
-                for h, a in enumerate(pair):
+                for a in pair:
                     if a != 0:
-                        home(q, h, j, me).wait_send()
-
-
-def last_kernel(plan, pieces, following, tab, update, new_momentum, through, sems):
+                        home(a, j, me).wait_send()
+
+
+def last_kernel(plan, pieces, following, tab, update, new_momentum, through, held, placed, sems):
     step = plan.rows // 4
     rows = [slice(i * step, (i + 1) * step) for i in range(4)]
+    fetch = pltpu.make_async_copy(pieces, held, sems.at[8])
     reads = [
         pltpu.make_async_copy(following.at[0, r], through.at[r], sems.at[i])
         for i, r in enumerate(rows)
@@ -439,19 +444,24 @@
         pltpu.make_async_copy(through.at[r], new_momentum.at[0, r], sems.at[4 + i])
         for i, r in enumerate(rows)
     ]
+    fetch.start()
     for read in reads:
         read.start()
+    fetch.wait()
 
     def place(b, c):
-        update[b] = pieces[tab[plan.where + b]]
+        placed[b] = held[tab[plan.where + b]]
         return c
 
     lax.fori_loop(0, plan.blocks, place, 0)
+    put = pltpu.make_async_copy(placed, update, sems.at[9])
+    put.start()
     for read, write in zip(reads, writes):
         read.wait()
         write.start()
     for write in writes:
         write.wait()
+    put.wait()
 
 
 def per_device(planes, groups, grads, left, right, momentum, block_order, owner_counts):
@@ -470,6 +480,7 @@
     anywhere = pl.BlockSpec(memory_space=pl.ANY)
     dma = pltpu.SemaphoreType.DMA
     held = plan.blocks + plan.sends
+    chunks = chunks_of(planes)
     pieces, following = pl.pallas_call(
         functools.partial(step_kernel, plan),
         out_shape=(
@@ -490,7 +501,7 @@
                 pltpu.VMEM((rows, cols), BF16),
                 pltpu.VMEM((rows, cols), F32),
                 pltpu.VMEM((rows, cols), BF16),
-                pltpu.VMEM((planes // 2, rows, 2 * width), BF16),
+                pltpu.VMEM((len(chunks), rows, 2 * width), BF16),
                 pltpu.VMEM((planes, groups, slab, width), BF16),
                 pltpu.VMEM((plan.slots, slab, width), BF16),
                 pltpu.VMEM((8, 128), F32),
@@ -509,12 +520,12 @@
                 dma,
                 dma((2,)),
                 dma((2,)),
-                dma((planes // 2,)),
-                dma((planes // 2,)),
+                dma((len(chunks),)),
+                dma((len(chunks),)),
                 dma((planes,)),
                 dma((planes,)),
             ]
-            + [pltpu.VMEM((groups, slab, 2 * width), BF16)] * (planes // 2)
+            + [pltpu.VMEM((groups, slab, len(c) * width), BF16) for c in chunks]
         ),
         compiler_params=pltpu.CompilerParams(
             collective_id=0, has_side_effects=True, vmem_limit_bytes=56 * 1024 * 1024
@@ -530,9 +541,14 @@
             jax.ShapeDtypeStruct((blocks, slab, width), BF16),
             jax.ShapeDtypeStruct((1, rows, cols), BF16),
         ),
-        in_specs=[pl.BlockSpec(memory_space=pltpu.VMEM), anywhere, smem],
-        out_specs=(pl.BlockSpec(memory_space=pltpu.VMEM), anywhere),
-        scratch_shapes=[pltpu.VMEM((rows, cols), BF16), dma((8,))],
+        in_specs=[anywhere, anywhere, smem],
+        out_specs=(anywhere, anywhere),
+        scratch_shapes=[
+            pltpu.VMEM((rows, cols), BF16),
+            pltpu.VMEM((plan.slots, slab, width), BF16),
+            pltpu.VMEM((blocks, slab, width), BF16),
+            dma((10,)),
+        ],
     )(pieces, following, table)
 
 

time: 165 us -> 162 us (0.982)
  Pallas kernels: 164 us -> 162 us
    pallas_call x1, Pallas kernels: 157 us -> 155 us  [per_device(): pl.pallas_call(functools.partial(step_kernel, plan), out_shape=(jax.Shape...]
where the time goes in v4:
time: 162 us
  Pallas kernels  162 us (100%)
    pallas_call x1, Pallas kernels, per_device(): pl.pallas_call(functools.partial(step_kernel, plan), out_shape=(jax.Shape...  155 us
    pallas_call x1, Pallas kernels, per_device(): pl.pallas_call(functools.partial(last_kernel, plan), out_shape=(jax.Shape...  3.79 us

profile of v4, /device:TPU:1, one launch (start us, length us, event | category | flops | bytes accessed | tf_op | source)
XLA Modules:
  0.0 162.1 jit_solution(16065581447052121330)
XLA Ops:
  0.6 2.6 %shard_map.77.tab = s32[314]{0:T(512)} custom-call(s32[64]{0:T(128)} %order_ref.1, s32[32]{0:T(128)} %counts_ref.1), custom_call_target="tpu_custom_call" | custom-call | tf_op jit(solution)/shard_map/pallas_call | solution.py:473
  3.2 155.1 %shard_map.78 = (bf16[102,32,128]{2,1,0:T(8,128)(2,1)}, bf16[1,1024,1024]{2,1,0:T(8,128)(2,1)}) custom-call(bf16[1,64,32,1024]{3,2,1,0:T(8,128)(2,1)} %grads.1, bf16[1,1024,1024]{2,1,0:T(8,128)(2,1)} %left.1, bf16[1,1024,1024]{2,1,0:T(8,128)(2,1)} %right.1, bf16[1,1024,1024]{2,1,0:T(8,128)(2,1)} %momentum.1, s32[314]{0:T(512)} %shard_map.77.tab), custom_call_target="tpu_custom_call" | custom-call | flops 4294967296 | bytes 13631488 | tf_op jit(solution)/shard_map/pallas_call | solution.py:484
  158.4 3.8 %shard_map.79 = (bf16[64,32,128]{2,1,0:T(8,128)(2,1)}, bf16[1,1024,1024]{2,1,0:T(8,128)(2,1)}) custom-call(bf16[102,32,128]{2,1,0:T(8,128)(2,1)} %get-tuple-element.4.pieces, bf16[1,1024,1024]{2,1,0:T(8,128)(2,1)} %get-tuple-element.5.following, s32[314]{0:T(512)} %shard_map.77.tab), custom_call_target="tpu_custom_call" | custom-call | tf_op jit(solution)/shard_map/pallas_call | solution.py:538

commit v5 on v4

--- a/solution.py
+++ b/solution.py
@@ -10,8 +10,8 @@
 MESH = pl.DeviceIdType.MESH
 LAG = 3
 PARTS = 1
-SKEW = 4
-EARLY = 20
+SKEW = 3
+EARLY = 18
 F32 = jnp.float32
 BF16 = jnp.bfloat16
 
@@ -124,6 +124,7 @@
     sq_own, sq_mid, sqz, sqs,
     load_sem, ring_send, ring_recv, z_send, zp_recv, zm_recv, a_send, a_recv,
     q_send, q_recv, u_send, u_recv, f_send, f_recv,
+    direct, zland, h_send, h_recv, g_send, g_recv,
     *rbufs,
 ):
     n, g, nb = plan.planes, plan.groups, plan.blocks
@@ -344,17 +345,18 @@
             f_send.at[a], f_recv.at[j], to, col,
         )
 
+    def step_of(at, a):
+        lanes = pl.ds(pl.multiple_of(lax.rem(me + a, n) * width, width), width)
+        direction = jnp.where(filled, clip * (graft * outer[at, lanes]), 0.0)
+        following = 0.9 * mv[at, lanes].astype(F32) + direction
+        nm[at, lanes] = following.astype(BF16)
+        return (-0.8 * (0.9 * following + direction)).astype(BF16)
+
     def outward(q, pair):
         def part(i):
             at = pl.ds(pl.multiple_of(i * tile, tile), tile)
             for h, a in enumerate(pair):
-                lanes = pl.ds(pl.multiple_of(lax.rem(me + a, n) * width, width), width)
-                direction = jnp.where(filled, clip * (graft * outer[at, lanes]), 0.0)
-                following = 0.9 * mv[at, lanes].astype(F32) + direction
-                nm[at, lanes] = following.astype(BF16)
-                ubuf[q, at, h * width:(h + 1) * width] = (
-                    -0.8 * (0.9 * following + direction)
-                ).astype(BF16)
+                ubuf[q, at, h * width:(h + 1) * width] = step_of(at, a)
 
         loop(0, rows // tile, part)
         rbufs[q][col] = ubuf[q, pl.ds(col * slab, slab), 0:len(pair) * width]
@@ -379,7 +381,7 @@
                 cbuf[a, r] = piece[:, h * width:(h + 1) * width]
 
         loop(0, g, gather)
-        for j in range(n):
+        for j in range(1, n):
             @pl.when(me == j)
             def _():
                 for a in pair:
@@ -390,18 +392,56 @@
                     else:
                         home(a, j, lax.rem(me + a, n)).start()
 
-    for q, pair in enumerate(pairs):
-        outward(q, pair)
-        if q > 0:
-            homeward(q - 1, pairs[q - 1])
     store = pltpu.make_async_copy(nm, new_momentum.at[0], load_sem.at[5])
-    store.start()
-    homeward(len(pairs) - 1, pairs[-1])
-
-    for j in range(n):
+
+    def across(a):
+        return remote(direct.at[a], zland, h_send.at[a], h_recv, lax.rem(me + a, n), col)
+
+    def scatter():
+        fbuf[col] = zland[pl.ds(col * slab, slab), :]
+
+        def drop(a):
+            to = lax.rem(col + a, g)
+            remote(
+                zland.at[pl.ds(to * slab, slab), :], fbuf.at[col], g_send, g_recv, me, to
+            ).start()
+
+        loop(1, g, drop)
+
+    @pl.when(me == 0)
+    def _():
+        for a in (a for pair in pairs for a in pair):
+            def part(i):
+                at = pl.ds(pl.multiple_of(i * tile, tile), tile)
+                if a == 0:
+                    zland[at, :] = step_of(at, a)
+                else:
+                    direct[a, at, :] = step_of(at, a)
+
+            loop(0, rows // tile, part)
+            if a != 0:
+                across(a).start()
+        store.start()
+        scatter()
+
+    @pl.when(me != 0)
+    def _():
+        for q, pair in enumerate(pairs):
+            outward(q, pair)
+            if q > 0:
+                homeward(q - 1, pairs[q - 1])
+        store.start()
+        across(0).wait_recv()
+        scatter()
+        homeward(len(pairs) - 1, pairs[-1])
+
+    for j in range(1, n):
         @pl.when(me != j)
         def _():
             home(0, j, me).wait_recv()
+
+    scattered = remote(fbuf.at[0:g - 1], fbuf.at[0:g - 1], g_send, g_recv, me, col)
+    scattered.wait_recv()
 
     keep = pltpu.make_async_copy(fbuf, pieces, load_sem.at[0])
     keep.start()
@@ -420,16 +460,25 @@
     remote(abuf.at[1:g], abuf.at[1:g], a_send, a_recv, me, col).wait_send()
     remote(sqz.at[0:n - 1], sqz.at[0:n - 1], q_send.at[0], q_recv.at[0], me, col).wait_send()
     remote(sqs.at[0:g - 1], sqs.at[0:g - 1], q_send.at[1], q_recv.at[1], me, col).wait_send()
-    for q, pair in enumerate(pairs):
-        remote(
-            rbufs[q].at[0:g - 1], rbufs[q].at[0:g - 1], u_send.at[q], u_recv.at[q], me, col
-        ).wait_send()
-        for j in range(n):
-            @pl.when(me == j)
-            def _():
-                for a in pair:
-                    if a != 0:
-                        home(a, j, me).wait_send()
+    scattered.wait_send()
+
+    @pl.when(me == 0)
+    def _():
+        for a in range(1, n):
+            across(a).wait_send()
+
+    @pl.when(me != 0)
+    def _():
+        for q in range(len(pairs)):
+            remote(
+                rbufs[q].at[0:g - 1], rbufs[q].at[0:g - 1], u_send.at[q], u_recv.at[q], me, col
+            ).wait_send()
+
+    for j in range(1, n):
+        @pl.when(me == j)
+        def _():
+            for a in range(1, n):
+                home(a, j, me).wait_send()
 
 
 def last_kernel(plan, pieces, following, tab, update, new_momentum, through, held, placed, sems):
@@ -524,6 +573,12 @@
                 dma((len(chunks),)),
                 dma((planes,)),
                 dma((planes,)),
+                pltpu.VMEM((planes, rows, width), BF16),
+                pltpu.VMEM((rows, width), BF16),
+                dma((planes,)),
+                dma,
+                dma,
+                dma,
             ]
             + [pltpu.VMEM((groups, slab, len(c) * width), BF16) for c in chunks]
         ),

time: 162 us -> 160 us (0.988)
  Pallas kernels: 162 us -> 160 us
    pallas_call x1, Pallas kernels: 155 us -> 153 us  [per_device(): pl.pallas_call(functools.partial(step_kernel, plan), out_shape=(jax.Shape...]
where the time goes in v5:
time: 160 us
  Pallas kernels  160 us (100%)
    pallas_call x1, Pallas kernels, per_device(): pl.pallas_call(functools.partial(step_kernel, plan), out_shape=(jax.Shape...  153 us
    pallas_call x1, Pallas kernels, per_device(): pl.pallas_call(functools.partial(last_kernel, plan), out_shape=(jax.Shape...  3.79 us

profile of v5, /device:TPU:1, one launch (start us, length us, event | category | flops | bytes accessed | tf_op | source)
XLA Modules:
  0.0 160.3 jit_solution(17573509513058377409)
XLA Ops:
  0.6 2.6 %shard_map.77.tab = s32[314]{0:T(512)} custom-call(s32[64]{0:T(128)} %order_ref.1, s32[32]{0:T(128)} %counts_ref.1), custom_call_target="tpu_custom_call" | custom-call | tf_op jit(solution)/shard_map/pallas_call | solution.py:522
  3.2 153.3 %shard_map.78 = (bf16[102,32,128]{2,1,0:T(8,128)(2,1)}, bf16[1,1024,1024]{2,1,0:T(8,128)(2,1)}) custom-call(bf16[1,64,32,1024]{3,2,1,0:T(8,128)(2,1)} %grads.1, bf16[1,1024,1024]{2,1,0:T(8,128)(2,1)} %left.1, bf16[1,1024,1024]{2,1,0:T(8,128)(2,1)} %right.1, bf16[1,1024,1024]{2,1,0:T(8,128)(2,1)} %momentum.1, s32[314]{0:T(512)} %shard_map.77.tab), custom_call_target="tpu_custom_call" | custom-call | flops 4294967296 | bytes 13631488 | tf_op jit(solution)/shard_map/pallas_call | solution.py:533
  156.5 3.8 %shard_map.79 = (bf16[64,32,128]{2,1,0:T(8,128)(2,1)}, bf16[1,1024,1024]{2,1,0:T(8,128)(2,1)}) custom-call(bf16[102,32,128]{2,1,0:T(8,128)(2,1)} %get-tuple-element.4.pieces, bf16[1,1024,1024]{2,1,0:T(8,128)(2,1)} %get-tuple-element.5.following, s32[314]{0:T(512)} %shard_map.77.tab), custom_call_target="tpu_custom_call" | custom-call | tf_op jit(solution)/shard_map/pallas_call | solution.py:593

commit v6 on v5

--- a/solution.py
+++ b/solution.py
@@ -46,6 +46,14 @@
     return [(n // 2,)] + [(n // 2 - i, n // 2 + i) for i in range(1, n // 2)] + [(0,)]
 
 
+def plane_order(n):
+    low, high = list(range(n // 2, 0, -1)), list(range(n // 2 + 1, n))
+    order = []
+    while high:
+        order += [high.pop(0), low.pop(0)]
+    return order + low + [0]
+
+
 def table_kernel(plan, order_ref, counts_ref, tab, held):
     n, g = plan.planes, plan.groups
     me, col = lax.axis_index("dp"), lax.axis_index("shard")
@@ -64,7 +72,7 @@
         b = order_ref[p]
         tab[plan.first + o] = b
         tab[plan.where + b] = o
-        tab[plan.rank + o] = jnp.where(k > me, mine, 0)
+        tab[plan.rank + o] = jnp.where(k > me, mine, -1)
         tab[plan.slot + o] = 0
         tab[plan.slot + mine] = o
         return p + k, mine + jnp.where(k > me, 1, 0)
@@ -121,7 +129,7 @@
     pieces, new_momentum,
     gp, gm, landp, landm, outp, outm, zp, zm, abuf, gblk,
     lv, rv, mv, inner, outer, nm, ubuf, cbuf, fbuf,
-    sq_own, sq_mid, sqz, sqs,
+    sq_own, sq_mid, sqz, sqs, sq_sum,
     load_sem, ring_send, ring_recv, z_send, zp_recv, zm_recv, a_send, a_recv,
     q_send, q_recv, u_send, u_recv, f_send, f_recv,
     direct, zland, h_send, h_recv, g_send, g_recv,
@@ -190,9 +198,7 @@
             held, land, _, _, _, start, sign, lag = way
             passing(way, k, h).wait_recv()
             own = held[tab[jnp.maximum(start + sign * (lag + k), 0)], :, parts[h]]
-            held[nb + k, :, parts[h]] = (
-                land[k, :, parts[h]].astype(F32) + own.astype(F32)
-            ).astype(BF16)
+            held[nb + k, :, parts[h]] = land[k, :, parts[h]] + own
 
     def give(k, h):
         for way in ways:
@@ -219,6 +225,10 @@
                 abuf.at[t], gblk.at[pl.ds(col * slab, slab), :], a_send, a_recv,
                 me, lax.rem(t + col, g),
             ).start()
+
+    def count_squares(t, counted):
+        x = abuf[t].astype(F32)
+        sq_sum[...] += jnp.where(counted, jnp.sum(x * x, axis=0, keepdims=True), 0.0)
 
     far = SKEW * (n - 1)
     lines = (
@@ -233,7 +243,7 @@
         return remote(zbuf.at[q], zbuf.at[q], z_send.at[d], recv.at[q], to, col)
 
     def first_block(line, q):
-        return line[0][tab[plan.first + lax.rem(q + col, g)]].astype(F32)
+        return line[0][tab[plan.first + lax.rem(q + col, g)]]
 
     def chain(t):
         @pl.when(me != 0)
@@ -246,12 +256,12 @@
                 def _():
                     @pl.when(me == source)
                     def _():
-                        zbuf[q] = first_block(line, q).astype(BF16)
+                        zbuf[q] = first_block(line, q)
 
                     @pl.when(me != source)
                     def _():
                         along(line, q).wait_recv()
-                        zbuf[q] = (zbuf[q].astype(F32) + first_block(line, q)).astype(BF16)
+                        zbuf[q] = zbuf[q] + first_block(line, q)
 
                     along(line, q).start()
 
@@ -260,54 +270,54 @@
             q = t - begin - far + LAG
             for line, low in zip(lines, (0, half)):
                 along(line, q).wait_recv()
-                abuf[q, low:low + half, :] = (
-                    line[1][q].astype(F32) + first_block(line, q)
-                ).astype(BF16)
+                abuf[q, low:low + half, :] = line[1][q] + first_block(line, q)
             exchange(q)
+            count_squares(q, True)
 
     def settle(t):
         i = t - ready
 
         @pl.when((i < g) & ((me != 0) | (i < LAG)))
         def _():
-            r = jnp.where(me == 0, i, tab[plan.rank + lax.rem(i + col, g)])
+            listed = tab[plan.rank + lax.rem(i + col, g)]
+            r = jnp.where(me == 0, i, jnp.maximum(listed, 0))
             abuf[i, 0:half, :] = gp[nb + tab[sc + 2] + r]
             abuf[i, half:slab, :] = gm[nb + tab[sc + 5] - r]
             exchange(i)
-
+            count_squares(i, listed >= 0)
+
+    sq_sum[...] = jnp.zeros_like(sq_sum)
     loop(0, LAG, lambda k: ring(k, taking=False))
     loop(LAG, begin, ring)
     loop(begin, plan.sends, lambda k: (ring(k), chain(k)))
     loop(plan.sends, ready, lambda k: (ring(k, giving=False), chain(k)))
     loop(ready, end, lambda k: (chain(k), settle(k)))
 
+    sq_own[...] = jnp.full((8, 128), jnp.sum(sq_sum[...]), F32)
+    sqz[me] = sq_own[...]
+    for a in range(1, n):
+        to = lax.rem(me + a, n)
+        remote(sq_own, sqz.at[me], q_send.at[0], q_recv.at[0], to, col).start()
+
     remote(
         gblk.at[0:(g - 1) * slab], gblk.at[0:(g - 1) * slab], a_send, a_recv, me, col
     ).wait_recv()
     filled = tab[sc + 6] > 0
     tile = min(128, rows)
-
-    def square(i, acc):
-        x = gblk[pl.ds(pl.multiple_of(i * tile, tile), tile), :].astype(F32)
-        return acc + jnp.sum(x * x, axis=0, keepdims=True)
-
-    grad_square = jnp.sum(lax.fori_loop(0, rows // tile, square, jnp.zeros((1, cols), F32)))
-    own_tile = jnp.full((8, 128), grad_square, F32)
-    sq_own[...] = jnp.where(filled, own_tile, 0.0)
-    sqz[me] = sq_own[...]
-    for a in range(1, n):
-        to = lax.rem(me + a, n)
-        remote(sq_own, sqz.at[me], q_send.at[0], q_recv.at[0], to, col).start()
     for load in loads:
         load.wait()
     strip = 256
 
-    def first_product(i, c):
+    def first_product(i, acc):
         at = pl.ds(pl.multiple_of(i * strip, strip), strip)
         inner[:, at] = jnp.dot(lv[...], gblk[:, at], preferred_element_type=F32).astype(BF16)
-        return c
-
-    lax.fori_loop(0, cols // strip, first_product, 0)
+        x = gblk[:, at].astype(F32)
+        return acc + jnp.sum(x * x, axis=0, keepdims=True)
+
+    grad_square = jnp.sum(
+        lax.fori_loop(0, cols // strip, first_product, jnp.zeros((1, strip), F32))
+    )
+    own_tile = jnp.full((8, 128), grad_square, F32)
     remote(sqz.at[0:n - 1], sqz.at[0:n - 1], q_send.at[0], q_recv.at[0], me, col).wait_recv()
     mid = sqz[0]
     for j in range(1, n):
@@ -410,7 +420,7 @@
 
     @pl.when(me == 0)
     def _():
-        for a in (a for pair in pairs for a in pair):
+        for a in plane_order(n):
             def part(i):
                 at = pl.ds(pl.multiple_of(i * tile, tile), tile)
                 if a == 0:
@@ -557,6 +567,7 @@
                 pltpu.VMEM((8, 128), F32),
                 pltpu.VMEM((planes, 8, 128), F32),
                 pltpu.VMEM((groups, 8, 128), F32),
+                pltpu.VMEM((1, cols), F32),
             ]
             + [
                 dma((6,)),

time: 160 us -> 159 us (level)
  no operation moved by 1% of the time
where the time goes in v6:
time: 159 us
  Pallas kernels  159 us (100%)
    pallas_call x1, Pallas kernels, per_device(): pl.pallas_call(functools.partial(step_kernel, plan), out_shape=(jax.Shape...  152 us
    pallas_call x1, Pallas kernels, per_device(): pl.pallas_call(functools.partial(last_kernel, plan), out_shape=(jax.Shape...  3.79 us

profile of v6, /device:TPU:1, one launch (start us, length us, event | category | flops | bytes accessed | tf_op | source)
XLA Modules:
  0.0 159.3 jit_solution(16455666772119669327)
XLA Ops:
  0.6 2.6 %shard_map.77.tab = s32[314]{0:T(512)} custom-call(s32[64]{0:T(128)} %order_ref.1, s32[32]{0:T(128)} %counts_ref.1), custom_call_target="tpu_custom_call" | custom-call | tf_op jit(solution)/shard_map/pallas_call | solution.py:532
  3.2 152.3 %shard_map.78 = (bf16[102,32,128]{2,1,0:T(8,128)(2,1)}, bf16[1,1024,1024]{2,1,0:T(8,128)(2,1)}) custom-call(bf16[1,64,32,1024]{3,2,1,0:T(8,128)(2,1)} %grads.1, bf16[1,1024,1024]{2,1,0:T(8,128)(2,1)} %left.1, bf16[1,1024,1024]{2,1,0:T(8,128)(2,1)} %right.1, bf16[1,1024,1024]{2,1,0:T(8,128)(2,1)} %momentum.1, s32[314]{0:T(512)} %shard_map.77.tab), custom_call_target="tpu_custom_call" | custom-call | flops 4294967296 | bytes 13631488 | tf_op jit(solution)/shard_map/pallas_call | solution.py:543
  155.5 3.8 %shard_map.79 = (bf16[64,32,128]{2,1,0:T(8,128)(2,1)}, bf16[1,1024,1024]{2,1,0:T(8,128)(2,1)}) custom-call(bf16[102,32,128]{2,1,0:T(8,128)(2,1)} %get-tuple-element.4.pieces, bf16[1,1024,1024]{2,1,0:T(8,128)(2,1)} %get-tuple-element.5.following, s32[314]{0:T(512)} %shard_map.77.tab), custom_call_target="tpu_custom_call" | custom-call | tf_op jit(solution)/shard_map/pallas_call | solution.py:604

commit v7 on v6

--- a/solution.py
+++ b/solution.py
@@ -10,8 +10,8 @@
 MESH = pl.DeviceIdType.MESH
 LAG = 3
 PARTS = 1
-SKEW = 3
-EARLY = 18
+SKEW = 2
+EARLY = 10
 F32 = jnp.float32
 BF16 = jnp.bfloat16
 

time: 159 us -> 176 us (1.11)
  Pallas kernels: 159 us -> 174 us
    pallas_call x1, Pallas kernels: 152 us -> 168 us  [per_device(): pl.pallas_call(functools.partial(step_kernel, plan), out_shape=(jax.Shape...]
where the time goes in v7:
time: 176 us; the launch traced here: 175 us
  Pallas kernels  174 us (99%)
    pallas_call x1, Pallas kernels, per_device(): pl.pallas_call(functools.partial(step_kernel, plan), out_shape=(jax.Shape...  168 us
    pallas_call x1, Pallas kernels, per_device(): pl.pallas_call(functools.partial(last_kernel, plan), out_shape=(jax.Shape...  3.79 us

profile of v7, /device:TPU:1, one launch (start us, length us, event | category | flops | bytes accessed | tf_op | source)
XLA Modules:
  0.0 174.8 jit_solution(7567264337852105597)
XLA Ops:
  0.6 2.6 %shard_map.77.tab = s32[314]{0:T(512)} custom-call(s32[64]{0:T(128)} %order_ref.1, s32[32]{0:T(128)} %counts_ref.1), custom_call_target="tpu_custom_call" | custom-call | tf_op jit(solution)/shard_map/pallas_call | solution.py:532
  3.2 167.8 %shard_map.78 = (bf16[102,32,128]{2,1,0:T(8,128)(2,1)}, bf16[1,1024,1024]{2,1,0:T(8,128)(2,1)}) custom-call(bf16[1,64,32,1024]{3,2,1,0:T(8,128)(2,1)} %grads.1, bf16[1,1024,1024]{2,1,0:T(8,128)(2,1)} %left.1, bf16[1,1024,1024]{2,1,0:T(8,128)(2,1)} %right.1, bf16[1,1024,1024]{2,1,0:T(8,128)(2,1)} %momentum.1, s32[314]{0:T(512)} %shard_map.77.tab), custom_call_target="tpu_custom_call" | custom-call | flops 4294967296 | bytes 13631488 | tf_op jit(solution)/shard_map/pallas_call | solution.py:543
  171.0 3.8 %shard_map.79 = (bf16[64,32,128]{2,1,0:T(8,128)(2,1)}, bf16[1,1024,1024]{2,1,0:T(8,128)(2,1)}) custom-call(bf16[102,32,128]{2,1,0:T(8,128)(2,1)} %get-tuple-element.4.pieces, bf16[1,1024,1024]{2,1,0:T(8,128)(2,1)} %get-tuple-element.5.following, s32[314]{0:T(512)} %shard_map.77.tab), custom_call_target="tpu_custom_call" | custom-call | tf_op jit(solution)/shard_map/pallas_call | solution.py:604

commit v8 on v7

--- a/solution.py
+++ b/solution.py
@@ -10,8 +10,8 @@
 MESH = pl.DeviceIdType.MESH
 LAG = 3
 PARTS = 1
-SKEW = 2
-EARLY = 10
+SKEW = 4
+EARLY = 24
 F32 = jnp.float32
 BF16 = jnp.bfloat16
 

time: 176 us -> 156 us (0.89)
  Pallas kernels: 174 us -> 155 us
    pallas_call x1, Pallas kernels: 168 us -> 149 us  [per_device(): pl.pallas_call(functools.partial(step_kernel, plan), out_shape=(jax.Shape...]
where the time goes in v8:
time: 156 us
  Pallas kernels  155 us (99%)
    pallas_call x1, Pallas kernels, per_device(): pl.pallas_call(functools.partial(step_kernel, plan), out_shape=(jax.Shape...  149 us
    pallas_call x1, Pallas kernels, per_device(): pl.pallas_call(functools.partial(last_kernel, plan), out_shape=(jax.Shape...  3.79 us

profile of v8, /device:TPU:1, one launch (start us, length us, event | category | flops | bytes accessed | tf_op | source)
XLA Modules:
  0.0 155.9 jit_solution(8545095303482313525)
XLA Ops:
  0.6 2.6 %shard_map.77.tab = s32[314]{0:T(512)} custom-call(s32[64]{0:T(128)} %order_ref.1, s32[32]{0:T(128)} %counts_ref.1), custom_call_target="tpu_custom_call" | custom-call | tf_op jit(solution)/shard_map/pallas_call | solution.py:532
  3.2 148.9 %shard_map.78 = (bf16[102,32,128]{2,1,0:T(8,128)(2,1)}, bf16[1,1024,1024]{2,1,0:T(8,128)(2,1)}) custom-call(bf16[1,64,32,1024]{3,2,1,0:T(8,128)(2,1)} %grads.1, bf16[1,1024,1024]{2,1,0:T(8,128)(2,1)} %left.1, bf16[1,1024,1024]{2,1,0:T(8,128)(2,1)} %right.1, bf16[1,1024,1024]{2,1,0:T(8,128)(2,1)} %momentum.1, s32[314]{0:T(512)} %shard_map.77.tab), custom_call_target="tpu_custom_call" | custom-call | flops 4294967296 | bytes 13631488 | tf_op jit(solution)/shard_map/pallas_call | solution.py:543
  152.1 3.8 %shard_map.79 = (bf16[64,32,128]{2,1,0:T(8,128)(2,1)}, bf16[1,1024,1024]{2,1,0:T(8,128)(2,1)}) custom-call(bf16[102,32,128]{2,1,0:T(8,128)(2,1)} %get-tuple-element.4.pieces, bf16[1,1024,1024]{2,1,0:T(8,128)(2,1)} %get-tuple-element.5.following, s32[314]{0:T(512)} %shard_map.77.tab), custom_call_target="tpu_custom_call" | custom-call | tf_op jit(solution)/shard_map/pallas_call | solution.py:604
